TPU v7x, 128 devices: a whole 4x4x4 slice. The times are simulated.
128 devices in a mesh: layer: 4 (over y), trace: 32 (over x, z, core).
Axes of the slice: x: 4, y: 4, z: 4, core: 2. Of those that a mesh axis runs over, the one named last changes fastest.
Arguments:
- pool_inputs: bfloat16 [4, 64, 128, 4096], P('layer', 'trace'), may hold values from -6 to 6
- val_inputs: bfloat16 [4, 64, 128, 4096], P('layer', 'trace'), may hold values from -6 to 6
- pool_top: bfloat16 [64, 128, 4096], P('trace'), may hold values from -6 to 6
- val_top: bfloat16 [64, 128, 4096], P('trace'), may hold values from -6 to 6
- weight: bfloat16 [4, 4096, 4096], P('layer', 'trace'), may hold values from -0.0625 to 0.0625
- proj_in: bfloat16 [4, 4096, 64], P('layer'), may hold values from -0.09375 to 0.09375
- proj_out: bfloat16 [4, 4096, 64], P('layer'), may hold values from -0.09375 to 0.09375
- pool_len: int32 [64], P('trace'), may hold values from 32 to 128, as said below
- val_len: int32 [64], P('trace'), may hold values from 32 to 128, as said below
Outputs:
- scores: float32 [64, 64], P('trace', 'layer')
Inputs may be any that keep to these rules, and one draw needn't show every extreme that they name: `pool_len`: every length lies in range and some pool trace and some validation trace have exactly 128 valid tokens. `val_len`: as for pool_len.
All inputs are finite; a program needn't handle non-finite values.
Results may differ from a plain program's by a relative error of at most 0.0056.
Values may be sent and summed in bfloat16 or wider, within the bound.
A program may use at most 192 MiB of HBM per device.

v0:
```python
import jax
import jax.numpy as jnp
from jax import lax
from jax.sharding import PartitionSpec as P


def passed_along(value, axis, steps):
    count = lax.axis_size(axis)
    first, last = (max(0, -steps), min(count, count - steps))
    return lax.ppermute(value, axis, [(source, source + steps) for source in range(first, last)])


def damped_inverse(factor):
    size_rank = factor.shape[0]
    identity = jnp.eye(size_rank, dtype=jnp.float32)
    damping = 0.1 * jnp.trace(factor) / size_rank
    lower_factor = jnp.linalg.cholesky(factor + damping * identity)
    return jax.scipy.linalg.cho_solve((lower_factor, True), identity)


def silu_slope(values):
    logistic = jax.nn.sigmoid(values)
    return logistic * (1.0 + values * (1.0 - logistic))


def pass_down(block):
    return passed_along(block, "layer", -1)


def on_device(
    pool_inputs, val_inputs, pool_top, val_top, weight, proj_in, proj_out, pool_len, val_len
):
    highest = lax.Precision.HIGHEST
    pool_local = pool_top.shape[0]
    val_local = val_top.shape[0]
    seq_tokens = pool_top.shape[1]
    model_width = pool_top.shape[2]
    rank_size = proj_in.shape[2]
    trace_local = pool_local + val_local
    section_index = lax.axis_index("layer")
    section_count = lax.axis_size("layer")
    full_weight = lax.all_gather(weight[0], "trace", axis=0, tiled=True)
    top_grads = jnp.concatenate([pool_top, val_top], 0)
    section_inputs = jnp.concatenate([pool_inputs[0], val_inputs[0]], 0)
    micro_count = 1
    block_traces = trace_local // micro_count

    def lower_grad(operands):
        block, input_block = operands
        flat_block = block.reshape(block_traces * seq_tokens, model_width)
        flat_inputs = input_block.reshape(block_traces * seq_tokens, model_width)
        gated = (
            flat_block.astype(jnp.float32) * silu_slope(flat_inputs.astype(jnp.float32))
        ).astype(jnp.bfloat16)
        lowered = flat_block.astype(jnp.float32) + jnp.dot(
            gated, full_weight, preferred_element_type=jnp.float32
        )
        return lowered.astype(jnp.bfloat16).reshape(block.shape)

    def skip_grad(operands):
        return jnp.zeros_like(operands[0])

    def chain_step(turn, carry):
        arrived, held_grads = carry
        slot_index = turn - (section_count - 1 - section_index)
        active = (slot_index >= 0) & (slot_index < micro_count)
        current = jnp.where(section_index == section_count - 1, top_grads, arrived)
        held_grads = jnp.where(active, current, held_grads)
        sent_block = lax.cond(
            active & (section_index > 0), lower_grad, skip_grad, (current, section_inputs)
        )
        return (pass_down(sent_block), held_grads)

    arrived_start = jnp.zeros((block_traces, seq_tokens, model_width), jnp.bfloat16)
    held_start = jnp.zeros_like(top_grads)
    _, held_grads = lax.fori_loop(
        0, section_count + micro_count - 1, chain_step, (arrived_start, held_start)
    )
    positions = jnp.arange(seq_tokens, dtype=jnp.int32)
    pool_mask = positions[None, :] < pool_len[:, None]
    val_mask = positions[None, :] < val_len[:, None]
    valid_mask = jnp.concatenate([pool_mask, val_mask], 0).astype(jnp.float32)
    layer_inputs = section_inputs.reshape(trace_local * seq_tokens, model_width)
    flat_grads = held_grads.reshape(trace_local * seq_tokens, model_width)
    grad_low = (
        jnp.dot(flat_grads, proj_out[0], preferred_element_type=jnp.float32).reshape(
            trace_local, seq_tokens, rank_size
        )
        * valid_mask[:, :, None]
    )
    input_low = (
        jnp.dot(layer_inputs, proj_in[0], preferred_element_type=jnp.float32).reshape(
            trace_local, seq_tokens, rank_size
        )
        * valid_mask[:, :, None]
    )
    trace_grads = jnp.einsum("nti,ntj->nij", grad_low, input_low, precision=highest)
    pool_grads = trace_grads[:pool_local]
    val_grads = trace_grads[pool_local:]
    pool_in = input_low[:pool_local].reshape(pool_local * seq_tokens, rank_size)
    pool_out = grad_low[:pool_local].reshape(pool_local * seq_tokens, rank_size)
    local_in = jnp.dot(pool_in.T, pool_in, precision=highest)
    local_out = jnp.dot(pool_out.T, pool_out, precision=highest)
    local_count = jnp.sum(pool_len).astype(jnp.float32)
    factor_in, factor_out, token_count = lax.psum((local_in, local_out, local_count), "trace")
    inv_in = damped_inverse(factor_in / token_count)
    inv_out = damped_inverse(factor_out / token_count)
    scaled = jnp.einsum("ab,nbc,cd->nad", inv_out, val_grads, inv_in, precision=highest)
    everything = lax.all_gather(
        scaled.reshape(val_local, rank_size * rank_size), "trace", axis=0, tiled=True
    )
    partial_scores = jnp.dot(
        pool_grads.reshape(pool_local, rank_size * rank_size), everything.T, precision=highest
    )
    summed = lax.psum_scatter(partial_scores, "layer", scatter_dimension=1, tiled=True)
    return summed / (rank_size * seq_tokens)


def solution(mesh):
    placed = (
        P("layer", "trace", None, None),
        P("layer", "trace", None, None),
        P("trace", None, None),
        P("trace", None, None),
        P("layer", "trace", None),
        P("layer", None, None),
        P("layer", None, None),
        P("trace"),
        P("trace"),
    )
    return jax.shard_map(
        on_device, mesh=mesh, in_specs=placed, out_specs=P("trace", "layer"), check_vma=False
    )
```

profile of v0, /device:TPU:8, one launch (start us, length us, event | category | flops | bytes accessed | tf_op | source)
XLA Modules:
  0.0 848.9 jit_solution(8215799855819495925)
XLA Ops:
  10.1 3.8 convolution_multiply_fusion
  15.4 3.6 pad_maximum_fusion
  19.0 106.9 %all-gather.5.cloned.1.call-done = bf16[1,4096,4096]{2,1,0:T(8,128)(2,1)} async-done(((bf16[1,128,4096]{2,1,0:T(8,128)(2,1)}), bf16[1,4096,4096]{2,1,0:T(8,128)(2,1)}) %all-gather.5.cloned.1.call-update) | async-done | bytes 33554448 | tf_op jit(solution)/shard_map/all_gather | solution.py:42
  125.9 2.5 broadcast.74
  128.5 491.8 %while.18 = (s32[]{:T(128)}, bf16[4,128,4096]{2,1,0:T(8,128)(2,1)}, bf16[4,128,4096]{2,1,0:T(8,128)(2,1)}, s32[]{:T(128)}, pred[]{:T(512)}, /*index=5*/pred[]{:T...) while((s32[]{:T(128)}, bf16[4,128,4096]{2,1,0:T(8,128)(2,1)}, ...), condition=%wide.region_3.4_spmd.clone, body=%wide.region_0.3_spmd.clone.sunk | while | flops 17215520768 | bytes 83886312 | solution.py:76
  128.5 5.2 select_select_fusion.4
  133.6 2.5 conditional.3
  133.6 2.5 broadcast.71
  136.1 2.4 collective-permute-start
  138.5 92.5 %collective-permute-done = bf16[4,128,4096]{2,1,0:T(8,128)(2,1)} collective-permute-done((bf16[4,128,4096]{2,1,0:T(8,128)(2,1)}, bf16[4,128,4096]{2,1,0:T(8,128)(2,1)}, u32[]{:S(2)}, u32[]{:S(2)}) %collective-permute-start) | collective-permute-done | bytes 4194336 | tf_op jit(solution)/shard_map/while/body/eval_jaxpr/ppermute | solution.py:10
  231.0 5.7 select_select_fusion.4
  236.8 2.5 conditional.3
  236.8 2.5 broadcast.71
  239.2 2.4 collective-permute-start
  241.7 147.1 %collective-permute-done = bf16[4,128,4096]{2,1,0:T(8,128)(2,1)} collective-permute-done((bf16[4,128,4096]{2,1,0:T(8,128)(2,1)}, bf16[4,128,4096]{2,1,0:T(8,128)(2,1)}, u32[]{:S(2)}, u32[]{:S(2)}) %collective-permute-start) | collective-permute-done | bytes 4194336 | tf_op jit(solution)/shard_map/while/body/eval_jaxpr/ppermute | solution.py:10
  388.8 5.7 select_select_fusion.4
  394.5 30.7 %conditional.3 = (bf16[4,128,4096]{2,1,0:T(8,128)(2,1)}) conditional(s32[]{:T(128)} %convert_element_type.59, () %tuple.56, (bf16[4,128,4096]{2,1,0:T(8,128)(2,1)}, bf16[4,128,4096]{2,1,0:T(8,128)(2,1)}, bf16[4096,4096]{1,0:T(8,128)(2,1)}) %tuple.57), branch_computations={%region_1.1_spmd, %region_2.2_spmd} | conditional | flops 17209229312 | bytes 46137352 | solution.py:69
  394.5 30.7 %fusion.1 = bf16[512,4096]{1,0:T(8,128)(2,1)} fusion(bf16[512,4096]{1,0:T(8,128)(2,1)} %bitcast.64, bf16[4096,4096]{1,0:T(8,128)(2,1)} %get-tuple-element.193, bf16[512,4096]{1,0:T(8,128)(2,1)} %bitcast.65), kind=kOutput, calls=%fused_computation.5 | convolution fusion | flops 17209229312 | bytes 46137344 | tf_op jit(solution)/shard_map/while/body/eval_jaxpr/cond/branch_1_fun/dot_general | solution.py:55
  427.1 92.0 %collective-permute-done = bf16[4,128,4096]{2,1,0:T(8,128)(2,1)} collective-permute-done((bf16[4,128,4096]{2,1,0:T(8,128)(2,1)}, bf16[4,128,4096]{2,1,0:T(8,128)(2,1)}, u32[]{:S(2)}, u32[]{:S(2)}) %collective-permute-start) | collective-permute-done | bytes 4194336 | tf_op jit(solution)/shard_map/while/body/eval_jaxpr/ppermute | solution.py:10
  519.1 5.7 select_select_fusion.4
  524.8 2.5 conditional.3
  524.8 2.5 broadcast.71
  527.3 2.2 collective-permute-start
  529.5 90.7 %collective-permute-done = bf16[4,128,4096]{2,1,0:T(8,128)(2,1)} collective-permute-done((bf16[4,128,4096]{2,1,0:T(8,128)(2,1)}, bf16[4,128,4096]{2,1,0:T(8,128)(2,1)}, u32[]{:S(2)}, u32[]{:S(2)}) %collective-permute-start) | collective-permute-done | bytes 4194336 | tf_op jit(solution)/shard_map/while/body/eval_jaxpr/ppermute | solution.py:10
  620.3 3.6 convolution_multiply_fusion.1
  624.5 124.5 %all-reduce = (f32[64,64]{0,1:T(8,128)S(1)}, f32[]{:T(128)}, f32[64,64]{0,1:T(8,128)S(1)}) all-reduce(f32[64,64]{0,1:T(8,128)S(1)} %convolution_bitcast_fusion.1, f32[]{:T(128)S(6)} %convert_element_type.45, f32[64,64]{0,1:T(8,128)S(1)} %copy-done.9), channel_id=1, replica_groups=mesh['layer'=4,'trace'=32] {'trace'}, use_global_device_ids=true, to_apply=%region_4.5 | all-reduce | flops 8193 | bytes 65544 | tf_op jit(solution)/shard_map/psum | solution.py:105
  752.4 5.8 cholesky.55
  759.6 4.9 custom-call.10
  768.3 5.8 cholesky.44
  775.5 4.9 custom-call.9
  782.1 37.6 %all-gather.7.cloned.1.call-done = f32[32,2,4096]{2,1,0:T(2,128)} async-done(((f32[1,2,4096]{2,1,0:T(2,128)}), f32[32,2,4096]{2,1,0:T(2,128)}) %all-gather.7.cloned.1.call-update) | async-done | bytes 1048592 | tf_op jit(solution)/shard_map/all_gather | solution.py:109
  823.3 17.8 %reduce-scatter.4.cloned.1.call-done = f32[16,2]{1,0:T(8,128)} async-done(((f32[64,2]{1,0:T(8,128)}), f32[16,2]{1,0:T(8,128)}) %reduce-scatter.4.cloned.1.call-update) | async-done | bytes 144
  (65 shorter events, 21.9 us)
Async XLA Ops:
  6.5 3.5 copy-start
  6.5 119.4 %all-gather.5.cloned.1.call-start = ((), (), s32[]{:S(2)}) async-start(), calls=%async_computation.1 | async-start | bytes 34603008 | tf_op jit(solution)/shard_map/all_gather | solution.py:42
  7.3 812.5 %all-gather.7.cloned.1.call-start = ((), (), s32[]{:S(2)}) async-start(), calls=%async_computation.2 | async-start | bytes 1081344 | tf_op jit(solution)/shard_map/all_gather | solution.py:109
  10.1 3.8 copy-start.10
  10.1 5.3 copy-start.2
  10.1 5.3 copy-start.3
  10.1 5.3 copy-start.4
  10.1 5.3 copy-start.5
  13.9 0.7 copy-start.6
  128.4 491.8 %copy-start.8 = (bf16[1,4096,64]{1,2,0:T(8,128)(2,1)S(1)}, bf16[1,4096,64]{1,2,0:T(8,128)(2,1)}, u32[]{:S(2)}) copy-start(bf16[1,4096,64]{1,2,0:T(8,128)(2,1)} %param.22) | copy-start | bytes 1572868
  128.4 491.8 %copy-start.11 = (f32[4,128]{1,0:T(4,128)S(1)}, f32[4,128]{1,0:T(4,128)}, u32[]{:S(2)}) copy-start(f32[4,128]{1,0:T(4,128)} %copy-done.10) | copy-start | bytes 6148
  136.1 94.9 %collective-permute-start = (bf16[4,128,4096]{2,1,0:T(8,128)(2,1)}, bf16[4,128,4096]{2,1,0:T(8,128)(2,1)}, u32[]{:S(2)}, u32[]{:S(2)}) collective-permute-start(bf16[4,128,4096]{2,1,0:T(8,128)(2,1)} %get-tuple-element.355), channel_id=1, source_target_pairs={{32,0},{64,32},{96,64},{33,1},{65,33},{97,65},{34,2},{66,34},{98,6... | collective-permute-start | bytes 12582920 | tf_op jit(solution)/shard_map/while/body/eval_jaxpr/ppermute | solution.py:10
  239.2 149.5 %collective-permute-start = (bf16[4,128,4096]{2,1,0:T(8,128)(2,1)}, bf16[4,128,4096]{2,1,0:T(8,128)(2,1)}, u32[]{:S(2)}, u32[]{:S(2)}) collective-permute-start(bf16[4,128,4096]{2,1,0:T(8,128)(2,1)} %get-tuple-element.355), channel_id=1, source_target_pairs={{32,0},{64,32},{96,64},{33,1},{65,33},{97,65},{34,2},{66,34},{98,6... | collective-permute-start | bytes 12582920 | tf_op jit(solution)/shard_map/while/body/eval_jaxpr/ppermute | solution.py:10
  425.2 93.9 %collective-permute-start = (bf16[4,128,4096]{2,1,0:T(8,128)(2,1)}, bf16[4,128,4096]{2,1,0:T(8,128)(2,1)}, u32[]{:S(2)}, u32[]{:S(2)}) collective-permute-start(bf16[4,128,4096]{2,1,0:T(8,128)(2,1)} %get-tuple-element.355), channel_id=1, source_target_pairs={{32,0},{64,32},{96,64},{33,1},{65,33},{97,65},{34,2},{66,34},{98,6... | collective-permute-start | bytes 12582920 | tf_op jit(solution)/shard_map/while/body/eval_jaxpr/ppermute | solution.py:10
  527.3 92.9 %collective-permute-start = (bf16[4,128,4096]{2,1,0:T(8,128)(2,1)}, bf16[4,128,4096]{2,1,0:T(8,128)(2,1)}, u32[]{:S(2)}, u32[]{:S(2)}) collective-permute-start(bf16[4,128,4096]{2,1,0:T(8,128)(2,1)} %get-tuple-element.355), channel_id=1, source_target_pairs={{32,0},{64,32},{96,64},{33,1},{65,33},{97,65},{34,2},{66,34},{98,6... | collective-permute-start | bytes 12582920 | tf_op jit(solution)/shard_map/while/body/eval_jaxpr/ppermute | solution.py:10
  620.2 3.9 copy-start.7
  620.2 4.2 copy-start.9
  620.2 222.2 %copy-start.1 = (bf16[1,4096,64]{1,2,0:T(8,128)(2,1)S(1)}, bf16[1,4096,64]{1,2,0:T(8,128)(2,1)}, u32[]{:S(2)}) copy-start(bf16[1,4096,64]{1,2,0:T(8,128)(2,1)} %param.21) | copy-start | bytes 1572868
  782.0 59.1 %reduce-scatter.4.cloned.1.call-start = ((), (), s32[]{:S(2)}) async-start(), calls=%async_computation.3 | async-start | bytes 40960
Sparse Core Ops, SparseCore 0:
  9.6 116.2 all-gather.4
  782.1 37.5 all-gather.6
  823.4 17.6 reduce-scatter.3
where the time goes:
time: 851 us; the launch traced here: 849 us
  waiting for transfers between devices  585 us (69%)
  blocking collectives  125 us (15%)
  other arithmetic  58.1 us (7%)
  matrix products  42.3 us (5%)
  between operations  15.3 us (2%)
  local copies, waits for them, and re-layouts  14.3 us (2%)
  starting transfers between devices  9.06 us (1%)
    ppermute x4, waiting for transfers between devices, passed_along(): lax.ppermute(value, axis, [(source, source + steps) for source in range(f...  422 us
    psum x1, blocking collectives, on_device(): lax.psum((local_in, local_out, local_count), 'trace')  125 us
    all_gather x1, waiting for transfers between devices, on_device(): full_weight = lax.all_gather(weight[0], 'trace', axis=0, tiled=True)  107 us
    all_gather x1, waiting for transfers between devices, on_device(): lax.all_gather(scaled.reshape(val_local, rank_size * rank_size), 'trace',...  37.6 us
    dot_general x1, matrix products, lower_grad(): jnp.dot(gated, full_weight, preferred_element_type=jnp.float32)  30.7 us
    select_n x4, other arithmetic, chain_step(): held_grads = jnp.where(active, current, held_grads)  22.4 us
    unnamed x4, waiting for transfers between devices  18.5 us
  transfers between devices with their start and end apart: 7, of which 7 were waited for; matrix products, arithmetic and copies ran while one was open for 1% of the time, Pallas kernels for 0%

commit v1 on v0

v1 whole, which is shorter than its diff:
```python
import functools

import jax
import jax.numpy as jnp
from jax import lax
from jax.experimental import pallas as pl
from jax.experimental.pallas import tpu as pltpu
from jax.sharding import PartitionSpec as P

MESH = pl.DeviceIdType.MESH
WIDTH = 4096
TOKENS = 128
CHUNKS = 16
COLS = WIDTH // CHUNKS
PAIRS = CHUNKS // 2
SHARE = 128
MAIN = 384
REST = 128
LAG_FORWARD, LAG_ROW, LAG_ROW_FORWARD, LAG_LAST, LAG_USE = 1, 2, 3, 4, 5
LAG_GRAD = 6
CATCH_UP = 3
SLOTS = 13


def silu_slope(values):
    logistic = jax.nn.sigmoid(values)
    return logistic * (1.0 + values * (1.0 - logistic))


def chain_kernel(
    pool_in, val_in, pool_top, val_top, weight,
    grad2_out, grad1_out, gated_out,
    held, first, second, gated, grad, total,
    send, recv, grad_send, grad_recv, act_send, act_recv, local, out_sem,
):
    layer = lax.axis_index("layer")
    trace = lax.axis_index("trace")
    x, z, c = trace // 8, (trace // 2) % 4, trace % 2
    xp, xm, xo = (x + 1) % 4, (x + 3) % 4, (x + 2) % 4
    zp, zm, zo = (z + 1) % 4, (z + 3) % 4, (z + 2) % 4
    other = 1 - c

    def at(xi, zi, ci):
        return {"trace": xi * 8 + zi * 2 + ci}

    above = {"layer": (layer + 1) % 4}
    below = {"layer": (layer + 3) % 4}

    barrier = pltpu.get_barrier_semaphore()
    for device in (at(xp, z, c), at(xm, z, c), at(x, zp, c), at(x, zm, c), at(x, z, other), above, below):
        pl.semaphore_signal(barrier, inc=1, device_id=device, device_id_type=MESH)
    pl.semaphore_wait(barrier, 7)

    def columns(j):
        return pl.ds(pl.multiple_of(j * COLS, COLS), COLS)

    def remote(src, dst, j, slot, device):
        return pltpu.make_async_remote_copy(
            src_ref=src, dst_ref=dst, send_sem=send.at[j, slot], recv_sem=recv.at[j, slot],
            device_id=device, device_id_type=MESH,
        )

    def arrived(ref, j, slot):
        remote(ref, ref, j, slot, at(x, z, other)).wait_recv()

    def push(ref, j, slot, device):
        remote(ref, ref, j, slot, device).start()

    def own(j):
        return held.at[j, x, z, c]

    def share_out(j, device):
        return remote(weight.at[:, columns(j)], own(j), j, 12, device)

    def share_local(j):
        return pltpu.make_async_copy(weight.at[:, columns(j)], own(j), local.at[j])

    def act_copy(src, dst, index, device):
        return pltpu.make_async_remote_copy(
            src_ref=src, dst_ref=dst, send_sem=act_send.at[index], recv_sem=act_recv.at[index],
            device_id=device, device_id_type=MESH,
        )

    def load(src, dst, index):
        return pltpu.make_async_copy(src, dst, local.at[CHUNKS + index])

    def loads(kind):
        if kind == 3:
            return [
                load(pool_in.at[0], first.at[0:128], 0), load(pool_in.at[1], first.at[128:256], 1),
                load(val_in.at[0], first.at[256:384], 2),
                load(pool_top.at[0], second.at[0:128], 3), load(pool_top.at[1], second.at[128:256], 4),
                load(val_top.at[0], second.at[256:384], 5),
            ]
        if kind == 2:
            return [
                load(pool_in.at[0], first.at[0:128], 0), load(pool_in.at[1], first.at[128:256], 1),
                load(val_in.at[0], first.at[256:384], 2),
            ]
        if kind == 1:
            return [load(val_in.at[1], second.at[0:128], 0)]
        return [load(val_top.at[1], second.at[0:128], 0)]

    def sends(kind):
        if kind == 3:
            return [act_copy(val_in.at[1], first.at[0:128], 0, above)]
        if kind == 2:
            return [act_copy(val_in.at[1], first.at[0:128], 0, below)]
        if kind == 1:
            return [
                act_copy(pool_in.at[0], second.at[0:128], 0, above),
                act_copy(pool_in.at[1], second.at[128:256], 1, above),
                act_copy(val_in.at[0], second.at[256:384], 2, above),
            ]
        return []

    def receives(kind):
        if kind == 2:
            return [act_copy(second.at[i * 128:(i + 1) * 128], second.at[i * 128:(i + 1) * 128], i, above) for i in range(3)]
        if kind in (0, 1):
            return [act_copy(first.at[0:128], first.at[0:128], 0, above)]
        return []

    @pl.when(layer >= 2)
    def _():
        def body(j, carry):
            share_local(j).start()
            return carry
        lax.fori_loop(0, CHUNKS, body, 0)

    for kind, partner in ((3, above), (2, below)):
        @pl.when(layer == kind)
        def _():
            for copy in loads(kind):
                copy.start()
            for j in range(4):
                share_out(j, partner).start()
            for copy in sends(kind):
                copy.start()
            for j in range(4, CHUNKS):
                share_out(j, partner).start()
    for kind in (1, 0):
        @pl.when(layer == kind)
        def _():
            for copy in loads(kind) + sends(kind):
                copy.start()

    def have_share(j):
        @pl.when(layer >= 2)
        def _():
            share_local(j).wait()

        @pl.when(layer < 2)
        def _():
            arrived(own(j), j, 12)

    half = SHARE // 2

    def stage_share(p):
        a, b = 2 * p, 2 * p + 1
        have_share(a)
        push(own(a), a, 0, at(xp, z, c))
        push(own(a), a, 1, at(xm, z, c))
        have_share(b)
        push(own(b), b, 0, at(x, zp, c))
        push(own(b), b, 1, at(x, zm, c))

    def stage_forward(p):
        a, b = 2 * p, 2 * p + 1
        arrived(held.at[a, xm, z, c], a, 0)
        push(held.at[a, xm, z, c, 0:half], a, 2, at(xp, z, c))
        arrived(held.at[b, x, zm, c], b, 0)
        push(held.at[b, x, zm, c, 0:half], b, 2, at(x, zp, c))
        arrived(held.at[a, xp, z, c], a, 1)
        push(held.at[a, xp, z, c, half:SHARE], a, 3, at(xm, z, c))
        arrived(held.at[b, x, zp, c], b, 1)
        push(held.at[b, x, zp, c, half:SHARE], b, 3, at(x, zm, c))

    def stage_row(p):
        a, b = 2 * p, 2 * p + 1
        arrived(held.at[a, xo, z, c, 0:half], a, 2)
        arrived(held.at[a, xo, z, c, half:SHARE], a, 3)
        push(held.at[a, :, z, c], a, 4, at(x, zp, c))
        push(held.at[a, :, z, c], a, 5, at(x, zm, c))
        arrived(held.at[b, x, zo, c, 0:half], b, 2)
        arrived(held.at[b, x, zo, c, half:SHARE], b, 3)
        push(held.at[b, x, :, c], b, 4, at(xp, z, c))
        push(held.at[b, x, :, c], b, 5, at(xm, z, c))
        push(held.at[a, :, z, c], a, 8, at(x, z, other))
        push(held.at[b, x, :, c], b, 8, at(x, z, other))

    def stage_row_forward(p):
        a, b = 2 * p, 2 * p + 1
        arrived(held.at[a, :, zm, c], a, 4)
        push(held.at[a, 0:2, zm, c], a, 6, at(x, zp, c))
        arrived(held.at[b, xm, :, c], b, 4)
        push(held.at[b, xm, 0:2, c], b, 6, at(xp, z, c))
        arrived(held.at[a, :, zp, c], a, 5)
        push(held.at[a, 2:4, zp, c], a, 7, at(x, zm, c))
        arrived(held.at[b, xp, :, c], b, 5)
        push(held.at[b, xp, 2:4, c], b, 7, at(xm, z, c))
        push(held.at[a, :, zm, c], a, 9, at(x, z, other))
        push(held.at[b, xm, :, c], b, 9, at(x, z, other))
        push(held.at[a, :, zp, c], a, 10, at(x, z, other))
        push(held.at[b, xp, :, c], b, 10, at(x, z, other))

    def stage_last(p):
        a, b = 2 * p, 2 * p + 1
        arrived(held.at[a, 0:2, zo, c], a, 6)
        arrived(held.at[a, 2:4, zo, c], a, 7)
        push(held.at[a, :, zo, c], a, 11, at(x, z, other))
        arrived(held.at[b, xo, 0:2, c], b, 6)
        arrived(held.at[b, xo, 2:4, c], b, 7)
        push(held.at[b, xo, :, c], b, 11, at(x, z, other))

    def stage_whole(p):
        a, b = 2 * p, 2 * p + 1
        for slot, zi in ((8, z), (9, zm), (10, zp), (11, zo)):
            arrived(held.at[a, :, zi, other], a, slot)
        for slot, xi in ((8, x), (9, xm), (10, xp), (11, xo)):
            arrived(held.at[b, xi, :, other], b, slot)

    def gate(rows, block):
        base = pl.multiple_of(block * 32, 32)
        value = first[pl.ds(base, 32), :].astype(jnp.float32)
        top = second[pl.ds(base, 32), :].astype(jnp.float32)
        gated[pl.ds(base, 32), :] = (top * silu_slope(value)).astype(jnp.bfloat16)

    def gate_all(rows):
        def body(block, carry):
            gate(rows, block)
            return carry
        lax.fori_loop(0, rows // 32, body, 0)

    def grad_copy(j, rows, device):
        return pltpu.make_async_remote_copy(
            src_ref=grad.at[j, 0:rows], dst_ref=grad.at[j, 0:rows],
            send_sem=grad_send.at[j], recv_sem=grad_recv.at[j],
            device_id=device, device_id_type=MESH,
        )

    def upper_chunk(j, rows, device):
        total[0, 0:rows] = second[0:rows, columns(j)].astype(jnp.float32)

        def body(xi, carry):
            block = held[j, xi].reshape(WIDTH // 4, COLS)
            left = gated[0:rows, pl.ds(pl.multiple_of(xi * (WIDTH // 4), WIDTH // 4), WIDTH // 4)]
            total[0, 0:rows] += jnp.dot(left, block, preferred_element_type=jnp.float32)
            return carry
        lax.fori_loop(0, 4, body, 0)
        grad[j, 0:rows] = total[0, 0:rows].astype(jnp.bfloat16)
        grad_copy(j, rows, device).start()

    def add_product(n, q, rows):
        block = held[n, q // 2, pl.ds(2 * (q % 2), 2)].reshape(4 * SHARE, COLS)
        left = gated[0:rows, pl.ds(pl.multiple_of(q * 2 * COLS, 2 * COLS), 2 * COLS)]
        total[n, 0:rows] += jnp.dot(left, block, preferred_element_type=jnp.float32)

    def lower_weight(n, ready, rows):
        total[n, 0:rows] = jnp.zeros((rows, COLS), jnp.float32)

        def body(k, carry):
            add_product(n, k, rows)
            return carry
        lax.fori_loop(0, ready, body, 0)

    def lower_grad(q, ready, rows):
        for k in (2 * q, 2 * q + 1):
            grad_copy(k, rows, above).wait_recv()

            def gating(block, carry):
                base = pl.multiple_of(block * 64, 64)
                value = first[pl.ds(base, 64), columns(k)].astype(jnp.float32)
                up = grad[k, pl.ds(base, 64)].astype(jnp.float32)
                gated[pl.ds(base, 64), columns(k)] = (up * silu_slope(value)).astype(jnp.bfloat16)
                return carry
            lax.fori_loop(0, rows // 64, gating, 0)

        def body(n, carry):
            add_product(n, q, rows)
            return carry
        lax.fori_loop(0, ready, body, 0)

    def upper_use(p, rows, device):
        upper_chunk(2 * p, rows, device)
        upper_chunk(2 * p + 1, rows, device)

    def lower_use(p, ready, rows):
        lower_weight(2 * p, ready, rows)
        lower_weight(2 * p + 1, ready, rows)

    def when_in(t, lag, what):
        @pl.when((t >= lag) & (t < PAIRS + lag))
        def _():
            what(t - lag)

    def step(t, carry):
        when_in(t, 0, stage_share)
        when_in(t, LAG_FORWARD, stage_forward)
        when_in(t, LAG_ROW, stage_row)
        when_in(t, LAG_ROW_FORWARD, stage_row_forward)
        when_in(t, LAG_LAST, stage_last)

        @pl.when((t == 0) & (layer == 3))
        def _():
            for copy in loads(3):
                copy.wait()
            gate_all(MAIN)

        @pl.when((t == 0) & (layer == 2))
        def _():
            for copy in loads(2):
                copy.wait()

        when_in(t, LAG_USE, stage_whole)

        @pl.when((t == LAG_USE + CATCH_UP) & (layer == 0))
        def _():
            for copy in loads(0):
                copy.wait()
            for copy in receives(0):
                copy.wait_recv()
            gate_all(REST)

            def body(j, carry):
                upper_chunk(j, REST, above)
                return carry
            lax.fori_loop(0, 2 * CATCH_UP, body, 0)

        @pl.when((t == LAG_USE) & (layer == 1))
        def _():
            for copy in loads(1):
                copy.wait()
            for copy in receives(1):
                copy.wait_recv()

        @pl.when((layer == 3) & (t >= LAG_USE) & (t < PAIRS + LAG_USE))
        def _():
            upper_use(t - LAG_USE, MAIN, below)

        @pl.when((layer == 0) & (t >= LAG_USE + CATCH_UP) & (t < PAIRS + LAG_USE))
        def _():
            upper_use(t - LAG_USE, REST, above)

        whole = jnp.minimum(2 * (t - LAG_USE) + 2, CHUNKS)

        @pl.when((layer == 2) & (t >= LAG_USE) & (t < PAIRS + LAG_USE))
        def _():
            lower_use(t - LAG_USE, jnp.maximum(t - LAG_GRAD, 0), MAIN)

        @pl.when((layer == 2) & (t >= LAG_GRAD) & (t < PAIRS + LAG_GRAD))
        def _():
            lower_grad(t - LAG_GRAD, whole, MAIN)

        first_rest = LAG_USE + CATCH_UP + 1

        @pl.when((layer == 1) & (t >= LAG_USE) & (t < PAIRS + LAG_USE))
        def _():
            since = jnp.maximum(t - first_rest, 0)
            lower_use(t - LAG_USE, jnp.where(since < 3, 2 * since, since + 3), REST)

        @pl.when((layer == 1) & (t >= first_rest) & (t < first_rest + 3))
        def _():
            q = 2 * (t - first_rest)
            lower_grad(q, whole, REST)
            lower_grad(q + 1, whole, REST)

        @pl.when((layer == 1) & (t >= first_rest + 3) & (t < first_rest + 5))
        def _():
            lower_grad(t - first_rest + 3, whole, REST)
        return carry

    lax.fori_loop(0, max(PAIRS + LAG_GRAD, LAG_USE + CATCH_UP + 6), step, 0)

    def finish(kind, rows):
        for copy in receives(kind) if kind == 2 else ():
            copy.wait_recv()

        def body(n, carry):
            def inner(block, inner_carry):
                base = pl.multiple_of(block * 64, 64)
                up = grad[n, pl.ds(base, 64)].astype(jnp.float32)
                value = second[pl.ds(base, 64), columns(n)].astype(jnp.float32)
                low = (up + total[n, pl.ds(base, 64)]).astype(jnp.bfloat16)
                first[pl.ds(base, 64), columns(n)] = low
                gated[pl.ds(base, 64), columns(n)] = (low.astype(jnp.float32) * silu_slope(value)).astype(jnp.bfloat16)
                return inner_carry
            lax.fori_loop(0, rows // 64, inner, 0)
            return carry
        lax.fori_loop(0, CHUNKS, body, 0)
        copies = [
            pltpu.make_async_copy(grad.at[:, 0:rows], grad2_out.at[:, 0:rows], out_sem.at[0]),
            pltpu.make_async_copy(first.at[0:rows], grad1_out.at[0:rows], out_sem.at[1]),
            pltpu.make_async_copy(gated.at[0:rows], gated_out.at[0:rows], out_sem.at[2]),
        ]
        for copy in copies:
            copy.start()
        for copy in copies:
            copy.wait()

    for kind, rows in ((2, MAIN), (1, REST)):
        @pl.when(layer == kind)
        def _():
            finish(kind, rows)

    def drain(p, carry):
        a, b = 2 * p, 2 * p + 1
        there = at(x, z, other)

        def left(ref, j, slot):
            remote(ref, ref, j, slot, there).wait_send()
        for slot in (0, 1):
            left(own(a), a, slot)
            left(own(b), b, slot)
        for slot in (2, 3):
            left(held.at[a, xm, z, c, 0:half], a, slot)
            left(held.at[b, x, zm, c, 0:half], b, slot)
        for slot in (4, 5, 8, 9, 10, 11):
            left(held.at[a, :, z, c], a, slot)
            left(held.at[b, x, :, c], b, slot)
        for slot in (6, 7):
            left(held.at[a, 0:2, z, c], a, slot)
            left(held.at[b, x, 0:2, c], b, slot)

        @pl.when(layer >= 2)
        def _():
            left(own(a), a, 12)
            left(own(b), b, 12)

        for kind, rows in ((3, MAIN), (0, REST)):
            @pl.when(layer == kind)
            def _():
                grad_copy(a, rows, above).wait_send()
                grad_copy(b, rows, above).wait_send()
        return carry
    lax.fori_loop(0, PAIRS, drain, 0)
    for kind in (3, 2, 1):
        @pl.when(layer == kind)
        def _():
            for copy in sends(kind):
                copy.wait_send()


def chain(pool_in, val_in, pool_top, val_top, weight):
    anywhere = pl.BlockSpec(memory_space=pl.ANY)
    wide = jax.ShapeDtypeStruct((MAIN, WIDTH), jnp.bfloat16)
    return pl.pallas_call(
        chain_kernel,
        out_shape=(jax.ShapeDtypeStruct((CHUNKS, MAIN, COLS), jnp.bfloat16), wide, wide),
        in_specs=[anywhere] * 5,
        out_specs=(anywhere,) * 3,
        scratch_shapes=[
            pltpu.VMEM((CHUNKS, 4, 4, 2, SHARE, COLS), jnp.bfloat16),
            pltpu.VMEM((MAIN, WIDTH), jnp.bfloat16),
            pltpu.VMEM((MAIN, WIDTH), jnp.bfloat16),
            pltpu.VMEM((MAIN, WIDTH), jnp.bfloat16),
            pltpu.VMEM((CHUNKS, MAIN, COLS), jnp.bfloat16),
            pltpu.VMEM((CHUNKS, MAIN, COLS), jnp.float32),
            pltpu.SemaphoreType.DMA((CHUNKS, SLOTS)),
            pltpu.SemaphoreType.DMA((CHUNKS, SLOTS)),
            pltpu.SemaphoreType.DMA((CHUNKS,)),
            pltpu.SemaphoreType.DMA((CHUNKS,)),
            pltpu.SemaphoreType.DMA((3,)),
            pltpu.SemaphoreType.DMA((3,)),
            pltpu.SemaphoreType.DMA((CHUNKS + 6,)),
            pltpu.SemaphoreType.DMA((3,)),
        ],
        compiler_params=pltpu.CompilerParams(
            collective_id=0, has_side_effects=True, vmem_limit_bytes=60 * 1024 * 1024
        ),
        cost_estimate=pl.CostEstimate(flops=26_000_000_000, bytes_accessed=30_000_000, transcendentals=3_000_000),
        name="chain",
    )(pool_in, val_in, pool_top, val_top, weight)


def damped_inverse(factor):
    size_rank = factor.shape[0]
    identity = jnp.eye(size_rank, dtype=jnp.float32)
    damping = 0.1 * jnp.trace(factor) / size_rank
    lower_factor = jnp.linalg.cholesky(factor + damping * identity)
    return jax.scipy.linalg.cho_solve((lower_factor, True), identity)


def sent(value, pairs):
    return lax.ppermute(value, "layer", pairs)


def on_device(
    pool_inputs, val_inputs, pool_top, val_top, weight, proj_in, proj_out, pool_len, val_len
):
    highest = lax.Precision.HIGHEST
    rank = proj_in.shape[2]
    pool_local, val_local = pool_top.shape[0], val_top.shape[0]
    layer = lax.axis_index("layer")
    f32 = jnp.float32

    projections = lax.all_gather(proj_out[0], "layer", axis=0)
    grad2, grad1, gated1 = chain(pool_inputs[0], val_inputs[0], pool_top, val_top, weight[0])
    folded = jnp.dot(weight[0], projections[0], preferred_element_type=f32).astype(jnp.bfloat16)
    folded = lax.all_gather(folded, "trace", axis=0, tiled=True)
    folded = jnp.where(layer == 2, sent(folded, [(1, 2)]), folded)

    flat_top = jnp.concatenate([pool_top, val_top], 0).reshape(-1, WIDTH)
    low_top = jnp.dot(flat_top, proj_out[0], preferred_element_type=f32)
    flat_inputs = jnp.concatenate([pool_inputs[0], val_inputs[0]], 0).reshape(-1, WIDTH)
    low_in = jnp.dot(flat_inputs, proj_in[0], preferred_element_type=f32)

    low2 = sum(
        jnp.dot(grad2[n], lax.dynamic_slice_in_dim(projections[2], n * COLS, COLS, 0), preferred_element_type=f32)
        for n in range(CHUNKS)
    )
    low1 = jnp.dot(grad1, projections[1], preferred_element_type=f32)
    low0 = jnp.dot(grad1, projections[0], preferred_element_type=f32) + jnp.dot(
        gated1, folded, preferred_element_type=f32
    )
    down = sent(jnp.where(layer == 2, low1, low0), [(2, 1), (1, 0)])
    up = sent(low2[:REST], [(1, 2)])
    far = sent(low0, [(2, 0)])
    main = jnp.where(layer == 2, low2, jnp.where(layer == 1, down, far))
    rest = jnp.where(layer == 2, up, jnp.where(layer == 1, low1[:REST], down[:REST]))
    low_out = jnp.where(layer == 3, low_top, jnp.concatenate([main, rest], 0))

    positions = jnp.arange(TOKENS, dtype=jnp.int32)
    lengths = jnp.concatenate([pool_len, val_len], 0)
    valid = positions[None, :] < lengths[:, None]
    grad_low = jnp.where(valid[:, :, None], low_out.reshape(-1, TOKENS, rank), 0.0)
    input_low = jnp.where(valid[:, :, None], low_in.reshape(-1, TOKENS, rank), 0.0)
    trace_grads = jnp.einsum("nti,ntj->nij", grad_low, input_low, precision=highest)
    pool_grads, val_grads = trace_grads[:pool_local], trace_grads[pool_local:]
    pool_in = input_low[:pool_local].reshape(-1, rank)
    pool_out = grad_low[:pool_local].reshape(-1, rank)
    local_in = jnp.dot(pool_in.T, pool_in, precision=highest)
    local_out = jnp.dot(pool_out.T, pool_out, precision=highest)
    local_count = jnp.sum(pool_len).astype(f32)
    factor_in, factor_out, token_count = lax.psum((local_in, local_out, local_count), "trace")
    inv_in = damped_inverse(factor_in / token_count)
    inv_out = damped_inverse(factor_out / token_count)
    scaled = jnp.einsum("ab,nbc,cd->nad", inv_out, val_grads, inv_in, precision=highest)
    everything = lax.all_gather(scaled.reshape(val_local, rank * rank), "trace", axis=0, tiled=True)
    partial_scores = jnp.dot(pool_grads.reshape(pool_local, rank * rank), everything.T, precision=highest)
    summed = lax.psum_scatter(partial_scores, "layer", scatter_dimension=1, tiled=True)
    return summed / (rank * TOKENS)


def solution(mesh):
    placed = (
        P("layer", "trace", None, None),
        P("layer", "trace", None, None),
        P("trace", None, None),
        P("trace", None, None),
        P("layer", "trace", None),
        P("layer", None, None),
        P("layer", None, None),
        P("trace"),
        P("trace"),
    )
    return jax.shard_map(
        on_device, mesh=mesh, in_specs=placed, out_specs=P("trace", "layer"), check_vma=False
    )
```

time: 851 us -> 463 us (0.54)
  waiting for transfers between devices: 585 us -> 60.6 us
  Pallas kernels: 0 us -> 167 us
  other arithmetic: 58.1 us -> 33.3 us
  blocking collectives: 125 us -> 148 us
  matrix products: 42.3 us -> 23.5 us
  local copies, waits for them, and re-layouts: 14.3 us -> 3.72 us
    ppermute x4, waiting for transfers between devices: 422 us -> 2.39 us  [sent(): return lax.ppermute(value, 'layer', pairs)]
    pallas_call x0 -> x1, Pallas kernels: none -> 167 us  [chain(): pl.pallas_call(chain_kernel, out_shape=(jax.ShapeDtypeStruct((CHUNKS, MAI...]
    all_gather x2, waiting for transfers between devices: 145 us -> 39.7 us  [the longest x1 39.7 us: on_device(): lax.all_gather(scaled.reshape(val_local, rank * rank), 'trace', axis=0, t...]
    all_gather x0 -> x1, blocking collectives: none -> 22.8 us  [on_device(): folded = lax.all_gather(folded, 'trace', axis=0, tiled=True)]
    select_n x4 -> x3, other arithmetic: 22.4 us -> 0.03 us  [the longest x1 0.02 us: on_device(): main = jnp.where(layer == 2, low2, jnp.where(layer == 1, down, far))]
    dot_general x3 -> x22, matrix products: 38.1 us -> 20 us  [the longest x16 9.86 us: on_device(): jnp.dot(grad2[n], lax.dynamic_slice_in_dim(projections[2], n * COLS, COLS...]
    another operation x4 -> x0, local copies, waits for them, and re-layouts: 9.94 us -> none
  transfers between devices with their start and end apart: 7 -> 7, of which waited for: 7 -> 5; matrix products, arithmetic and copies ran while one was open for 1% -> 5% of each run, Pallas kernels for 0% -> 36%
where the time goes in v1:
time: 463 us; the launch traced here: 461 us
  Pallas kernels  167 us (36%)
  blocking collectives  148 us (32%)
  waiting for transfers between devices  60.6 us (13%)
  other arithmetic  33.3 us (7%)
  matrix products  23.5 us (5%)
  between operations  15.4 us (3%)
  starting transfers between devices  8.82 us (2%)
    pallas_call x1, Pallas kernels, chain(): pl.pallas_call(chain_kernel, out_shape=(jax.ShapeDtypeStruct((CHUNKS, MAI...  167 us
    psum x1, blocking collectives, on_device(): lax.psum((local_in, local_out, local_count), 'trace')  126 us
    all_gather x1, waiting for transfers between devices, on_device(): lax.all_gather(scaled.reshape(val_local, rank * rank), 'trace', axis=0, t...  39.7 us
    all_gather x1, blocking collectives, on_device(): folded = lax.all_gather(folded, 'trace', axis=0, tiled=True)  22.8 us
    unnamed x4, waiting for transfers between devices  18.5 us
    another operation x6, other arithmetic, damped_inverse(): lower_factor = jnp.linalg.cholesky(factor + damping * identity)  13 us
    another operation x4, other arithmetic, damped_inverse(): return jax.scipy.linalg.cho_solve((lower_factor, True), identity)  11.1 us
    dot_general x16, matrix products, on_device(): jnp.dot(grad2[n], lax.dynamic_slice_in_dim(projections[2], n * COLS, COLS...  9.86 us
  transfers between devices with their start and end apart: 7, of which 5 were waited for; matrix products, arithmetic and copies ran while one was open for 5% of the time, Pallas kernels for 36%

profile of v1, /device:TPU:8, one launch (start us, length us, event | category | flops | bytes accessed | tf_op | source)
XLA Modules:
  0.0 460.7 jit_solution(10178945797433352938)
XLA Ops:
  8.1 3.8 fusion.4
  13.4 3.9 pad_maximum_fusion
  17.3 167.0 %chain.1 = (bf16[16,384,256]{2,1,0:T(8,128)(2,1)}, bf16[384,4096]{1,0:T(8,128)(2,1)}, bf16[384,4096]{1,0:T(8,128)(2,1)}) custom-call(bf16[2,128,4096]{2,1,0:T(8,128)(2,1)} %bitcast.177, bf16[2,128,4096]{2,1,0:T(8,128)(2,1)} %bitcast.179, bf16[2,128,4096]{2,1,0:T(8,128)(2,1)} %pool_top.1, bf16[2,128,4096]{2,1,0:T(8,128)(2,1)} %val_top.1, ...), custom_call_target="tpu_custom_call" | custom-call | flops 25999998976 | bytes 30000000 | tf_op jit(solution)/shard_map/chain/pallas_call | solution.py:447
  184.4 1.7 convolution_convert_fusion
  186.1 22.8 %all_gather.10 = bf16[4096,64]{0,1:T(8,128)(2,1)S(1)} all-gather(bf16[128,64]{0,1:T(8,128)(2,1)S(1)} %convolution_convert_fusion), channel_id=1, replica_groups=mesh['layer'=4,'trace'=32] {'trace'}, dimensions={0}, use_global_device_ids=true | all-gather | bytes 540672 | tf_op jit(solution)/shard_map/all_gather | solution.py:500
  208.9 1.3 collective-permute-start
  210.2 1.3 fusion.29
  211.5 1.1 convolution_add_fusion.15
  212.6 1.1 convolution_add_fusion.14
  213.7 1.0 convolution_add_fusion.13
  214.7 1.0 convolution_add_fusion.12
  215.7 1.0 convolution_add_fusion.11
  216.6 1.0 convolution_add_fusion.10
  220.0 1.1 fusion.13
  221.1 1.0 collective-permute-done
  222.1 1.1 convolution_add_fusion
  224.0 1.1 broadcast_select_fusion
  225.1 1.9 collective-permute-start.1
  227.3 4.7 %collective-permute-start.3 = (f32[128,64]{0,1:T(8,128)S(1)}, f32[128,64]{0,1:T(8,128)S(1)}, u32[]{:S(2)}, u32[]{:S(2)}) collective-permute-start(f32[128,64]{0,1:T(8,128)S(1)} %slice.163), channel_id=1, source_target_pairs={{32,64},{33,65},{34,66},{35,67},{36,68},{37,69},{38,70},{39,71},{4... | collective-permute-start | bytes 98312 | tf_op jit(solution)/shard_map/ppermute | solution.py:485
  232.4 1.0 collective-permute-done.3
  233.4 1.4 fusion.47
  235.4 125.5 %all-reduce = (f32[64,64]{0,1:T(8,128)S(1)}, f32[]{:T(128)}, f32[64,64]{0,1:T(8,128)S(1)}) all-reduce(f32[64,64]{0,1:T(8,128)S(1)} %convolution_bitcast_fusion.1, f32[]{:T(128)S(6)} %convert_element_type.13, f32[64,64]{0,1:T(8,128)S(1)} %convolution_bitcast_fusion), channel_id=1, replica_groups=mesh['layer'=4,'trace'=32] {'trace'}, use_global_device_ids=true, to_apply=%region_0.1 | all-reduce | flops 8193 | bytes 65544 | tf_op jit(solution)/shard_map/psum | solution.py:535
  360.9 1.3 select_reduce_fusion.3
  362.2 1.2 select_reduce_fusion.2
  365.4 5.8 %cholesky.55 = f32[64,64]{1,0:T(8,128)S(1)} custom-call(f32[64,64]{1,0:T(8,128)S(1)} %fusion.59), custom_call_target="Cholesky" | custom-call | tf_op jit(solution)/shard_map/jit(cholesky)/cholesky | solution.py:480
  372.6 4.9 %custom-call.9 = f32[1,64,64]{1,2,0:T(8,128)S(1)} custom-call(f32[1,64,64]{2,1,0:T(8,128)S(1)} %fusion.55), custom_call_target="InvertDiagBlocksLowerTriangular" | custom-call | tf_op jit(solution)/shard_map/jit(_cho_solve)/triangular_solve | solution.py:481
  378.0 5.8 %cholesky.44 = f32[64,64]{1,0:T(8,128)S(1)} custom-call(f32[64,64]{1,0:T(8,128)S(1)} %fusion.62), custom_call_target="Cholesky" | custom-call | tf_op jit(solution)/shard_map/jit(cholesky)/cholesky | solution.py:480
  385.2 4.9 %custom-call.8 = f32[1,64,64]{1,2,0:T(8,128)S(1)} custom-call(f32[1,64,64]{2,1,0:T(8,128)S(1)} %fusion.54), custom_call_target="InvertDiagBlocksLowerTriangular" | custom-call | tf_op jit(solution)/shard_map/jit(_cho_solve)/triangular_solve | solution.py:481
  391.8 39.7 %all-gather.6.cloned.1.call-done = f32[32,2,4096]{2,1,0:T(2,128)} async-done(((f32[1,2,4096]{2,1,0:T(2,128)}), f32[32,2,4096]{2,1,0:T(2,128)}) %all-gather.6.cloned.1.call-update) | async-done | bytes 1048592 | tf_op jit(solution)/shard_map/all_gather | solution.py:539
  431.5 1.9 reshape.70
  433.4 1.6 convolution_bitcast_fusion.2
  435.0 17.8 %reduce-scatter.4.cloned.1.call-done = f32[16,2]{1,0:T(8,128)} async-done(((f32[64,2]{1,0:T(8,128)}), f32[16,2]{1,0:T(8,128)}) %reduce-scatter.4.cloned.1.call-update) | async-done | bytes 144
  (71 shorter events, 13.7 us)
Async XLA Ops:
  6.5 1.6 copy-start
  6.5 177.8 %all-gather.4.cloned.1.call-start = ((), (), s32[]{:S(2)}) async-start(), calls=%async_computation.1 | async-start | bytes 2621440 | tf_op jit(solution)/shard_map/all_gather | solution.py:497
  7.3 424.2 %all-gather.6.cloned.1.call-start = ((), (), s32[]{:S(2)}) async-start(), calls=%async_computation.2 | async-start | bytes 1081344 | tf_op jit(solution)/shard_map/all_gather | solution.py:539
  8.1 3.8 copy-start.9
  8.1 5.3 %copy-start.6 = (bf16[2,128,4096]{2,1,0:T(8,128)(2,1)S(1)}, bf16[2,128,4096]{2,1,0:T(8,128)(2,1)}, u32[]{:S(2)}) copy-start(bf16[2,128,4096]{2,1,0:T(8,128)(2,1)} %pool_top.1) | copy-start | bytes 6291460
  17.3 167.0 %copy-start.8 = (bf16[1,128,4096]{2,1,0:T(8,128)(2,1)S(1)}, bf16[1,128,4096]{2,1,0:T(8,128)(2,1)}, u32[]{:S(2)}) copy-start(bf16[1,128,4096]{2,1,0:T(8,128)(2,1)} %param.16) | copy-start | bytes 3145732
  184.4 29.4 %copy-start.4 = (bf16[16,384,256]{2,1,0:T(8,128)(2,1)S(1)}, bf16[16,384,256]{2,1,0:T(8,128)(2,1)}, u32[]{:S(2)}) copy-start(bf16[16,384,256]{2,1,0:T(8,128)(2,1)} %get-tuple-element.10) | copy-start | bytes 9437188
  184.4 34.2 %copy-start.7 = (bf16[4,4096,64]{1,2,0:T(8,128)(2,1)S(1)}, bf16[4,4096,64]{1,2,0:T(8,128)(2,1)}, u32[]{:S(2)}) copy-start(bf16[4,4096,64]{1,2,0:T(8,128)(2,1)} %all-gather.4.cloned.1.call-done) | copy-start | bytes 6291460
  208.9 13.3 %collective-permute-start = (bf16[4096,64]{0,1:T(8,128)(2,1)S(1)}, bf16[4096,64]{0,1:T(8,128)(2,1)S(1)}, u32[]{:S(2)}, u32[]{:S(2)}) collective-permute-start(bf16[4096,64]{0,1:T(8,128)(2,1)S(1)} %all_gather.10), channel_id=1, source_target_pairs={{32,64},{33,65},{34,66},{35,67},{36,68},{37,69},{38,70},{39,71},{4... | collective-permute-start | bytes 1572872 | tf_op jit(solution)/shard_map/ppermute | solution.py:485
  210.2 9.8 %copy-start.1 = (bf16[384,4096]{1,0:T(8,128)(2,1)S(1)}, bf16[384,4096]{1,0:T(8,128)(2,1)}, u32[]{:S(2)}) copy-start(bf16[384,4096]{1,0:T(8,128)(2,1)} %get-tuple-element.11) | copy-start | bytes 9437188
  219.4 2.7 copy-start.3
  223.2 10.2 %copy-start.2 = (bf16[4,128,4096]{2,1,0:T(8,128)(2,1)S(1)}, bf16[4,128,4096]{2,1,0:T(8,128)(2,1)}, u32[]{:S(2)}) copy-start(bf16[4,128,4096]{2,1,0:T(8,128)(2,1)} %pad_maximum_fusion) | copy-start | bytes 12582916
  223.2 10.2 %copy-start.5 = (bf16[1,4096,64]{1,2,0:T(8,128)(2,1)S(1)}, bf16[1,4096,64]{1,2,0:T(8,128)(2,1)}, u32[]{:S(2)}) copy-start(bf16[1,4096,64]{1,2,0:T(8,128)(2,1)} %param.18) | copy-start | bytes 1572868
  223.2 9.2 %collective-permute-start.2 = (f32[384,64]{0,1:T(8,128)S(1)}, f32[384,64]{0,1:T(8,128)S(1)}, u32[]{:S(2)}, u32[]{:S(2)}) collective-permute-start(f32[384,64]{0,1:T(8,128)S(1)} %convolution_add_fusion), channel_id=1, source_target_pairs={{64,0},{65,1},{66,2},{67,3},{68,4},{69,5},{70,6},{71,7},{72,8},{73... | collective-permute-start | bytes 294920 | tf_op jit(solution)/shard_map/ppermute | solution.py:485
  225.1 7.3 %collective-permute-start.1 = (f32[384,64]{0,1:T(8,128)S(1)}, f32[384,64]{0,1:T(8,128)S(1)}, u32[]{:S(2)}, u32[]{:S(2)}) collective-permute-start(f32[384,64]{0,1:T(8,128)S(1)} %get-tuple-element.16), channel_id=1, source_target_pairs={{64,32},{32,0},{65,33},{33,1},{66,34},{34,2},{67,35},{35,3},{68,36... | collective-permute-start | bytes 294920 | tf_op jit(solution)/shard_map/ppermute | solution.py:485
  227.3 6.1 %collective-permute-start.3 = (f32[128,64]{0,1:T(8,128)S(1)}, f32[128,64]{0,1:T(8,128)S(1)}, u32[]{:S(2)}, u32[]{:S(2)}) collective-permute-start(f32[128,64]{0,1:T(8,128)S(1)} %slice.163), channel_id=1, source_target_pairs={{32,64},{33,65},{34,66},{35,67},{36,68},{37,69},{38,70},{39,71},{4... | collective-permute-start | bytes 98312 | tf_op jit(solution)/shard_map/ppermute | solution.py:485
  391.6 61.2 %reduce-scatter.4.cloned.1.call-start = ((), (), s32[]{:S(2)}) async-start(), calls=%async_computation.3 | async-start | bytes 40960
Sparse Core Ops, SparseCore 0:
  9.0 48.9 all-gather.3
  391.8 39.6 all-gather.5
  435.1 17.6 reduce-scatter.3

commit v2 on v1

--- a/solution.py
+++ b/solution.py
@@ -10,6 +10,7 @@
 MESH = pl.DeviceIdType.MESH
 WIDTH = 4096
 TOKENS = 128
+RANK = 64
 CHUNKS = 16
 COLS = WIDTH // CHUNKS
 PAIRS = CHUNKS // 2
@@ -473,12 +474,212 @@
     )(pool_in, val_in, pool_top, val_top, weight)
 
 
-def damped_inverse(factor):
-    size_rank = factor.shape[0]
-    identity = jnp.eye(size_rank, dtype=jnp.float32)
-    damping = 0.1 * jnp.trace(factor) / size_rank
-    lower_factor = jnp.linalg.cholesky(factor + damping * identity)
-    return jax.scipy.linalg.cho_solve((lower_factor, True), identity)
+def low_half(shape):
+    return lax.broadcasted_iota(jnp.int32, shape, len(shape) - 1) < RANK
+
+
+def damped_inverses(pair):
+    rows = lax.broadcasted_iota(jnp.int32, pair.shape, 0)
+    lanes = lax.broadcasted_iota(jnp.int32, pair.shape, 1)
+    lower = lanes < RANK
+    column = jnp.where(lower, lanes, lanes - RANK)
+    diagonal = rows == column
+    on_diagonal = jnp.where(diagonal, pair, 0.0)
+    trace_first = jnp.sum(jnp.where(lower, on_diagonal, 0.0), keepdims=True)
+    trace_second = jnp.sum(jnp.where(lower, 0.0, on_diagonal), keepdims=True)
+    damping = jnp.where(lower, trace_first, trace_second) * (0.1 / RANK)
+    value = jnp.where(diagonal, pair + damping, pair)
+    for k in range(RANK):
+        left = jnp.where(
+            lower,
+            jnp.broadcast_to(value[:, k:k + 1], pair.shape),
+            jnp.broadcast_to(value[:, RANK + k:RANK + k + 1], pair.shape),
+        )
+        pivot = 1.0 / left[k:k + 1]
+        row = jnp.where(column[k:k + 1] == k, pivot, value[k:k + 1] * pivot)
+        left = jnp.where(rows == k, -1.0, left)
+        value = jnp.where((rows == k) | (column == k), 0.0, value) - left * row
+    return value
+
+
+def score_kernel(
+    top_low, mid_low, in_low, counts, scores_out,
+    landed, factors, factors_z, vals, layers,
+    low_send, low_recv, fac_send, fac_recv, val_send, val_recv, facz_send, facz_recv, valz_send, valz_recv,
+    lay_send, lay_recv,
+):
+    layer = lax.axis_index("layer")
+    trace = lax.axis_index("trace")
+    x, z, c = trace // 8, (trace // 2) % 4, trace % 2
+    highest = lax.Precision.HIGHEST
+    f32, bf16 = jnp.float32, jnp.bfloat16
+
+    near = []
+    for dx in range(4):
+        for dc in range(2):
+            if dx or dc:
+                xi, ci = (x + dx) % 4, (c + dc) % 2
+                near.append((xi * 2 + ci, xi, ci, {"trace": xi * 8 + z * 2 + ci}))
+    across = [((z + dz) % 4, {"trace": x * 8 + (z + dz) % 4 * 2 + c}) for dz in (1, 3, 2)]
+    planes = [((layer + dl) % 4, {"layer": (layer + dl) % 4}) for dl in (1, 3, 2)]
+    barrier = pltpu.get_barrier_semaphore()
+    for device in [n[3] for n in near] + [a[1] for a in across] + [q[1] for q in planes]:
+        pl.semaphore_signal(barrier, inc=1, device_id=device, device_id_type=MESH)
+    pl.semaphore_wait(barrier, len(near) + len(across) + len(planes))
+
+    def copy(src, dst, send, recv, device):
+        return pltpu.make_async_remote_copy(
+            src_ref=src, dst_ref=dst, send_sem=send, recv_sem=recv, device_id=device, device_id_type=MESH
+        )
+
+    def low(source, slot, plane):
+        return copy(source, landed.at[slot], low_send.at[slot + 3 * plane], low_recv.at[slot], {"layer": plane})
+
+    def lows(kind):
+        if kind == 2:
+            return [low(mid_low.at[1, 0], 0, 1), low(mid_low.at[1, 1], 1, 1),
+                    low(mid_low.at[0, 0], 0, 0), low(mid_low.at[0, 1], 1, 0)]
+        if kind == 1:
+            return [low(mid_low.at[0, 1], 2, 0), low(mid_low.at[2, 1], 2, 2)]
+        return []
+
+    def lows_in(kind):
+        return [low(landed.at[slot], slot, (kind + 1) % 4) for slot in {3: (), 2: (2,), 1: (0, 1), 0: (0, 1, 2)}[kind]]
+
+    for kind in (2, 1):
+        @pl.when(layer == kind)
+        def _():
+            for item in lows(kind):
+                item.start()
+
+    @pl.when(layer == 3)
+    def _():
+        landed[0] = top_low[0]
+        landed[1] = top_low[1]
+        landed[2] = jnp.zeros_like(landed[2])
+
+    @pl.when(layer == 2)
+    def _():
+        landed[0] = mid_low[2, 0]
+        landed[1] = mid_low[2, 1]
+
+    @pl.when(layer == 1)
+    def _():
+        landed[2] = mid_low[1, 1]
+
+    for kind in (2, 1, 0):
+        @pl.when(layer == kind)
+        def _():
+            for item in lows_in(kind):
+                item.wait_recv()
+
+    def across_tokens(left, right):
+        return lax.dot_general(left, right, (((0,), (0,)), ((), ())), precision=highest, preferred_element_type=f32)
+
+    wide = (RANK, 2 * RANK)
+    lower = low_half(wide)
+
+    def blocks(value):
+        return jnp.where(lower, value[0:RANK], value[RANK:2 * RANK])
+
+    def both(value):
+        return value + pltpu.roll(value, RANK, 1)
+
+    pool_out = landed[0].astype(f32)
+    val_out = landed[1].astype(f32) + landed[2].astype(f32)
+    pool_in, val_in = in_low[0], in_low[1]
+    vals[x, z, c] = blocks(across_tokens(val_out, val_in)).astype(bf16)
+    part_in = both(blocks(across_tokens(pool_in, pool_in)))
+    part_out = both(blocks(across_tokens(pool_out, pool_out)))
+    factors[x * 2 + c, 0:RANK] = jnp.where(lower, part_in, part_out)
+    factors[x * 2 + c, RANK:RANK + 8] = counts[...]
+
+    mine = x * 2 + c
+    first = [copy(factors.at[mine], factors.at[mine], fac_send.at[i], fac_recv.at[mine], n[3]) for i, n in enumerate(near)]
+    first += [copy(vals.at[x, z, c], vals.at[x, z, c], val_send.at[i], val_recv.at[mine], n[3]) for i, n in enumerate(near)]
+    for item in first:
+        item.start()
+    pool_grads = blocks(across_tokens(pool_in, pool_out))
+    for slot, xi, ci, device in near:
+        copy(factors.at[slot], factors.at[slot], fac_send.at[0], fac_recv.at[slot], device).wait_recv()
+    factors_z[z] = sum(factors[i] for i in range(1, 8)) + factors[0]
+    second = [copy(factors_z.at[z], factors_z.at[z], facz_send.at[i], facz_recv.at[z], a[1]) for i, a in enumerate(across)]
+    for item in second:
+        item.start()
+    for slot, xi, ci, device in near:
+        copy(vals.at[xi, z, ci], vals.at[xi, z, ci], val_send.at[0], val_recv.at[slot], device).wait_recv()
+    third = [copy(vals.at[:, z], vals.at[:, z], valz_send.at[i], valz_recv.at[z], a[1]) for i, a in enumerate(across)]
+    for item in third:
+        item.start()
+    for zi, device in across:
+        copy(factors_z.at[zi], factors_z.at[zi], facz_send.at[0], facz_recv.at[zi], device).wait_recv()
+    total = factors_z[0] + factors_z[1] + factors_z[2] + factors_z[3]
+    inverse = damped_inverses(total[0:RANK] / total[RANK:RANK + 1])
+    inv_in = inverse[:, 0:RANK]
+    turned = pltpu.roll(inverse, RANK, 1)
+    twice = jnp.where(lower, turned, inverse)
+    inv_out = jnp.concatenate([jnp.where(lower, twice, 0.0), jnp.where(lower, 0.0, twice)], 0)
+    scaled = jnp.dot(inv_in, pool_grads, precision=highest, preferred_element_type=f32)
+    scaled = jnp.dot(scaled, inv_out, precision=highest, preferred_element_type=f32)
+    coarse = scaled.astype(bf16)
+    fine = (scaled - coarse.astype(f32)).astype(bf16)
+    empty = jnp.zeros(wide, bf16)
+
+    def spread(value):
+        return jnp.concatenate(
+            [jnp.concatenate([value, empty], 1), jnp.concatenate([empty, value], 1)], 0
+        )
+
+    coarse, fine = spread(coarse), spread(fine)
+    for zi, device in across:
+        copy(vals.at[:, zi], vals.at[:, zi], valz_send.at[0], valz_recv.at[zi], device).wait_recv()
+    every = vals[...].reshape(32 * RANK, 2 * RANK)
+    product = jnp.dot(every, coarse, preferred_element_type=f32) + jnp.dot(every, fine, preferred_element_type=f32)
+    at_row = lax.broadcasted_iota(jnp.int32, product.shape, 0) % RANK
+    at_lane = lax.broadcasted_iota(jnp.int32, product.shape, 1) % RANK
+    summed = jnp.where(at_row == at_lane, product, 0.0).reshape(32, RANK, 4 * RANK).sum(1)
+    group = lax.broadcasted_iota(jnp.int32, (8, 4 * RANK), 1) // RANK
+    picks = (lax.broadcasted_iota(jnp.int32, (8, 4 * RANK), 0) == group).astype(f32)
+    part = lax.dot_general(picks, summed, (((1,), (1,)), ((), ())), precision=highest, preferred_element_type=f32)
+    layers[layer] = jnp.concatenate([part, jnp.zeros((8, 96), f32)], 1)
+    last = [copy(layers.at[layer], layers.at[layer], lay_send.at[i], lay_recv.at[layer], q[1]) for i, q in enumerate(planes)]
+    for item in last:
+        item.start()
+    for plane, device in planes:
+        copy(layers.at[plane], layers.at[plane], lay_send.at[0], lay_recv.at[plane], device).wait_recv()
+    scores_out[...] = (layers[0] + layers[1] + layers[2] + layers[3]) * (1.0 / (RANK * TOKENS))
+
+    for item in first + second + third + last:
+        item.wait_send()
+    for kind in (2, 1):
+        @pl.when(layer == kind)
+        def _():
+            for item in lows(kind):
+                item.wait_send()
+
+
+def score(top_low, mid_low, in_low, counts):
+    inside = pl.BlockSpec(memory_space=pltpu.VMEM)
+    dma = pltpu.SemaphoreType.DMA
+    return pl.pallas_call(
+        score_kernel,
+        out_shape=jax.ShapeDtypeStruct((8, 128), jnp.float32),
+        in_specs=[inside] * 4,
+        out_specs=inside,
+        scratch_shapes=[
+            pltpu.VMEM((3, TOKENS, 2 * RANK), jnp.bfloat16),
+            pltpu.VMEM((8, RANK + 8, 2 * RANK), jnp.float32),
+            pltpu.VMEM((4, RANK + 8, 2 * RANK), jnp.float32),
+            pltpu.VMEM((4, 4, 2, RANK, 2 * RANK), jnp.bfloat16),
+            pltpu.VMEM((4, 8, 128), jnp.float32),
+            dma((12,)), dma((3,)), dma((7,)), dma((8,)), dma((7,)), dma((8,)),
+            dma((3,)), dma((4,)), dma((3,)), dma((4,)), dma((3,)), dma((4,)),
+        ],
+        compiler_params=pltpu.CompilerParams(
+            collective_id=1, has_side_effects=True, vmem_limit_bytes=32 * 1024 * 1024
+        ),
+        name="score",
+    )(top_low, mid_low, in_low, counts)
 
 
 def sent(value, pairs):
@@ -488,9 +689,7 @@
 def on_device(
     pool_inputs, val_inputs, pool_top, val_top, weight, proj_in, proj_out, pool_len, val_len
 ):
-    highest = lax.Precision.HIGHEST
     rank = proj_in.shape[2]
-    pool_local, val_local = pool_top.shape[0], val_top.shape[0]
     layer = lax.axis_index("layer")
     f32 = jnp.float32
 
@@ -513,33 +712,23 @@
     low0 = jnp.dot(grad1, projections[0], preferred_element_type=f32) + jnp.dot(
         gated1, folded, preferred_element_type=f32
     )
-    down = sent(jnp.where(layer == 2, low1, low0), [(2, 1), (1, 0)])
-    up = sent(low2[:REST], [(1, 2)])
-    far = sent(low0, [(2, 0)])
-    main = jnp.where(layer == 2, low2, jnp.where(layer == 1, down, far))
-    rest = jnp.where(layer == 2, up, jnp.where(layer == 1, low1[:REST], down[:REST]))
-    low_out = jnp.where(layer == 3, low_top, jnp.concatenate([main, rest], 0))
-
     positions = jnp.arange(TOKENS, dtype=jnp.int32)
     lengths = jnp.concatenate([pool_len, val_len], 0)
-    valid = positions[None, :] < lengths[:, None]
-    grad_low = jnp.where(valid[:, :, None], low_out.reshape(-1, TOKENS, rank), 0.0)
-    input_low = jnp.where(valid[:, :, None], low_in.reshape(-1, TOKENS, rank), 0.0)
-    trace_grads = jnp.einsum("nti,ntj->nij", grad_low, input_low, precision=highest)
-    pool_grads, val_grads = trace_grads[:pool_local], trace_grads[pool_local:]
-    pool_in = input_low[:pool_local].reshape(-1, rank)
-    pool_out = grad_low[:pool_local].reshape(-1, rank)
-    local_in = jnp.dot(pool_in.T, pool_in, precision=highest)
-    local_out = jnp.dot(pool_out.T, pool_out, precision=highest)
-    local_count = jnp.sum(pool_len).astype(f32)
-    factor_in, factor_out, token_count = lax.psum((local_in, local_out, local_count), "trace")
-    inv_in = damped_inverse(factor_in / token_count)
-    inv_out = damped_inverse(factor_out / token_count)
-    scaled = jnp.einsum("ab,nbc,cd->nad", inv_out, val_grads, inv_in, precision=highest)
-    everything = lax.all_gather(scaled.reshape(val_local, rank * rank), "trace", axis=0, tiled=True)
-    partial_scores = jnp.dot(pool_grads.reshape(pool_local, rank * rank), everything.T, precision=highest)
-    summed = lax.psum_scatter(partial_scores, "layer", scatter_dimension=1, tiled=True)
-    return summed / (rank * TOKENS)
+    valid = (positions[None, :] < lengths[:, None])[:, :, None]
+
+    def packed(low):
+        low = jnp.where(valid, low.reshape(4, TOKENS, rank), 0.0)
+        return jnp.stack([jnp.concatenate([low[0], low[1]], 1), jnp.concatenate([low[2], low[3]], 1)])
+
+    def spread(low):
+        main = jnp.where(layer == 2, low, 0.0)
+        return packed(jnp.concatenate([main, jnp.where(layer == 1, low[:REST], 0.0)], 0))
+
+    mid_low = jnp.stack([spread(low0), spread(low1), spread(low2)]).astype(jnp.bfloat16)
+    counts = jnp.full((8, 2 * rank), jnp.sum(pool_len).astype(f32))
+    summed = score(packed(low_top).astype(jnp.bfloat16), mid_low, packed(low_in), counts)
+    table = summed[:4, :32].reshape(2, 2, 32).transpose(1, 2, 0).reshape(2, 64)
+    return lax.dynamic_slice_in_dim(table, layer * 16, 16, 1)
 
 
 def solution(mesh):

time: 463 us -> 267 us (0.58)
  blocking collectives: 148 us -> 23.2 us
  waiting for transfers between devices: 60.6 us -> 0.73 us
  other arithmetic: 33.3 us -> 3.69 us
  Pallas kernels: 167 us -> 194 us
  starting transfers between devices: 8.82 us -> 2.09 us
    psum x1 -> x0, blocking collectives: 126 us -> none  [on_device(): lax.psum((local_in, local_out, local_count), 'trace')]
    all_gather x1 -> x0, waiting for transfers between devices: 39.7 us -> none  [on_device(): lax.all_gather(scaled.reshape(val_local, rank * rank), 'trace', axis=0, t...]
    pallas_call x0 -> x1, Pallas kernels: none -> 27 us  [score(): pl.pallas_call(score_kernel, out_shape=jax.ShapeDtypeStruct((8, 128), jnp...]
    another operation x10 -> x15, other arithmetic: 24.1 us -> 0.95 us  [the longest x10 0.73 us: packed(): jnp.stack([jnp.concatenate([low[0], low[1]], 1), jnp.concatenate([low[2],...]
    unnamed x4 -> x1, waiting for transfers between devices: 18.5 us -> 0.71 us
    ppermute x4 -> x1, starting transfers between devices: 8.73 us -> 2.09 us  [sent(): return lax.ppermute(value, 'layer', pairs)]
  transfers between devices with their start and end apart: 7 -> 2, of which waited for: 5 -> 0; matrix products, arithmetic and copies ran while one was open for 5% -> 10% of each run, Pallas kernels for 36% -> 63%
where the time goes in v2:
time: 267 us; the launch traced here: 265 us
  Pallas kernels  194 us (73%)
  matrix products  23.7 us (9%)
  blocking collectives  23.2 us (9%)
  between operations  14.5 us (5%)
  other arithmetic  3.69 us (1%)
  local copies, waits for them, and re-layouts  3.62 us (1%)
    pallas_call x1, Pallas kernels, chain(): pl.pallas_call(chain_kernel, out_shape=(jax.ShapeDtypeStruct((CHUNKS, MAI...  166 us
    pallas_call x1, Pallas kernels, score(): pl.pallas_call(score_kernel, out_shape=jax.ShapeDtypeStruct((8, 128), jnp...  27 us
    all_gather x1, blocking collectives, on_device(): folded = lax.all_gather(folded, 'trace', axis=0, tiled=True)  23.2 us
    dot_general x16, matrix products, on_device(): jnp.dot(grad2[n], lax.dynamic_slice_in_dim(projections[2], n * COLS, COLS...  9.87 us
  transfers between devices with their start and end apart: 2, of which 0 were waited for; matrix products, arithmetic and copies ran while one was open for 10% of the time, Pallas kernels for 63%

profile of v2, /device:TPU:8, one launch (start us, length us, event | category | flops | bytes accessed | tf_op | source)
XLA Modules:
  0.0 265.0 jit_solution(4080648963430881129)
XLA Ops:
  6.5 0.7 all-gather.2.cloned.1.call-update
  7.3 0.7 pad_add_fusion
  8.1 3.7 %fusion.14 = bf16[4,128,64]{2,1,0:T(8,128)(2,1)S(1)} fusion(bf16[2,128,4096]{2,1,0:T(8,128)(2,1)} %val_top.1, bf16[2,128,4096]{2,1,0:T(8,128)(2,1)} %pool_top.1, bf16[1,4096,64]{1,2,0:T(8,128)(2,1)} %param.15, pred[4,128]{1,0:T(4,128)(4,1)S(1)} %iota_compare_fusion), kind=kOutput, calls=%fused_computation.10 | convolution fusion | flops 270598144 | bytes 4784640 | tf_op jit(solution)/shard_map/dot_general | solution.py:703
  11.8 0.6 reduce_sum.9
  13.2 2.8 %fusion.8 = f32[4,128,64]{2,1,0:T(8,128)S(1)} fusion(bf16[2,128,4096]{2,1,0:T(8,128)(2,1)} %bitcast.204, bf16[2,128,4096]{2,1,0:T(8,128)(2,1)S(1)} %bitcast.203, bf16[1,4096,64]{1,2,0:T(8,128)(2,1)S(1)} %copy-done, pred[4,128]{1,0:T(4,128)(4,1)S(1)} %iota_compare_fusion), kind=kOutput, calls=%fused_computation.8 | convolution fusion | flops 270565376 | bytes 4850176 | tf_op jit(solution)/shard_map/dot_general | solution.py:705
  16.2 166.5 %chain.1 = (bf16[16,384,256]{2,1,0:T(8,128)(2,1)}, bf16[384,4096]{1,0:T(8,128)(2,1)}, bf16[384,4096]{1,0:T(8,128)(2,1)}) custom-call(bf16[2,128,4096]{2,1,0:T(8,128)(2,1)} %bitcast.202, bf16[2,128,4096]{2,1,0:T(8,128)(2,1)} %bitcast.205, bf16[2,128,4096]{2,1,0:T(8,128)(2,1)} %pool_top.1, bf16[2,128,4096]{2,1,0:T(8,128)(2,1)} %val_top.1, ...), custom_call_target="tpu_custom_call" | custom-call | flops 25999998976 | bytes 30000000 | tf_op jit(solution)/shard_map/chain/pallas_call | solution.py:448
  182.7 2.0 convolution_convert_fusion
  184.7 23.2 %all_gather.7 = bf16[4096,64]{0,1:T(8,128)(2,1)S(1)} all-gather(bf16[128,64]{0,1:T(8,128)(2,1)S(1)} %convolution_convert_fusion), channel_id=1, replica_groups=mesh['layer'=4,'trace'=32] {'trace'}, dimensions={0}, use_global_device_ids=true | all-gather | bytes 540672 | tf_op jit(solution)/shard_map/all_gather | solution.py:699
  207.9 2.1 collective-permute-start
  210.0 1.1 fusion.38
  211.1 1.3 convolution_add_fusion.14
  212.4 1.1 convolution_add_fusion.13
  213.6 1.0 convolution_add_fusion.12
  214.5 1.0 convolution_add_fusion.11
  215.5 1.0 convolution_add_fusion.10
  216.4 1.0 convolution_add_fusion.9
  217.4 1.0 convolution_add_fusion.8
  218.4 0.2 convolution_add_fusion.7
  218.8 0.2 convolution_add_fusion.5
  219.2 0.2 convolution_add_fusion.3
  219.4 0.2 convolution_add_fusion.2
  219.6 0.2 convolution_add_fusion.1
  219.8 0.2 broadcast_select_fusion
  220.0 1.1 broadcast_select_fusion.1
  221.1 0.6 pad_maximum_fusion.3
  221.8 1.0 copy.25
  222.7 0.6 pad_maximum_fusion.2
  223.4 1.6 copy.24
  225.0 3.1 %fusion.22 = f32[384,64]{0,1:T(8,128)S(1)} fusion(bf16[384,4096]{1,0:T(8,128)(2,1)} %get-tuple-element.8, bf16[4,4096,64]{1,2,0:T(8,128)(2,1)S(1)} %copy-done.4), kind=kOutput, calls=%fused_computation.35 | convolution fusion | flops 201326592 | bytes 3768320 | tf_op jit(solution)/shard_map/dot_general | solution.py:712
  228.1 1.1 broadcast_select_fusion.2
  230.3 27.0 %score.1 = f32[8,128]{1,0:T(8,128)S(1)} custom-call(bf16[2,128,128]{2,1,0:T(8,128)(2,1)S(1)} %pad_maximum_fusion.5.top_low, bf16[3,2,128,128]{3,2,1,0:T(8,128)(2,1)S(1)} %pad_maximum_fusion.mid_low, f32[2,128,128]{2,1,0:T(8,128)S(1)} %pad_maximum_fusion.4.in_low, f32[8,128]{1,0:T(8,128)S(1)} %broadcast_in_dim.50.counts), custom_call_target="tpu_custom_call" | custom-call | tf_op jit(solution)/shard_map/score/pallas_call | solution.py:664
  257.5 0.6 constant_dynamic-slice_fusion
  (50 shorter events, 1.9 us)
Async XLA Ops:
  6.5 6.7 %copy-start = (bf16[1,4096,64]{1,2,0:T(8,128)(2,1)S(1)}, bf16[1,4096,64]{1,2,0:T(8,128)(2,1)}, u32[]{:S(2)}) copy-start(bf16[1,4096,64]{1,2,0:T(8,128)(2,1)} %param.14) | copy-start | bytes 1572868
  6.5 176.2 %all-gather.2.cloned.1.call-start = ((), (), s32[]{:S(2)}) async-start(), calls=%async_computation | async-start | bytes 2621440 | tf_op jit(solution)/shard_map/all_gather | solution.py:696
  8.1 3.7 %copy-start.7 = (s32[2]{0:T(128)S(1)}, s32[2]{0:T(128)}, u32[]{:S(2)}) copy-start(s32[2]{0:T(128)} %param.16) | copy-start | bytes 28
  8.1 5.1 %copy-start.6 = (bf16[1,2,128,4096]{3,2,1,0:T(8,128)(2,1)S(1)}, bf16[1,2,128,4096]{3,2,1,0:T(8,128)(2,1)}, u32[]{:S(2)}) copy-start(bf16[1,2,128,4096]{3,2,1,0:T(8,128)(2,1)} %param.9) | copy-start | bytes 6291460
  182.7 30.8 %copy-start.3 = (bf16[16,384,256]{2,1,0:T(8,128)(2,1)S(1)}, bf16[16,384,256]{2,1,0:T(8,128)(2,1)}, u32[]{:S(2)}) copy-start(bf16[16,384,256]{2,1,0:T(8,128)(2,1)} %get-tuple-element.10) | copy-start | bytes 9437188
  182.7 35.6 %copy-start.4 = (bf16[4,4096,64]{1,2,0:T(8,128)(2,1)S(1)}, bf16[4,4096,64]{1,2,0:T(8,128)(2,1)}, u32[]{:S(2)}) copy-start(bf16[4,4096,64]{1,2,0:T(8,128)(2,1)} %all-gather.2.cloned.1.call-done) | copy-start | bytes 6291460
  207.9 20.2 %collective-permute-start = (bf16[4096,64]{0,1:T(8,128)(2,1)S(1)}, bf16[4096,64]{0,1:T(8,128)(2,1)}, u32[]{:S(2)}, u32[]{:S(2)}) collective-permute-start(bf16[4096,64]{0,1:T(8,128)(2,1)S(1)} %all_gather.7), channel_id=1, source_target_pairs={{32,64},{33,65},{34,66},{35,67},{36,68},{37,69},{38,70},{39,71},{4... | collective-permute-start | bytes 1572872 | tf_op jit(solution)/shard_map/ppermute | solution.py:686
  211.1 8.9 %copy-start.1 = (bf16[384,4096]{1,0:T(8,128)(2,1)S(1)}, bf16[384,4096]{1,0:T(8,128)(2,1)}, u32[]{:S(2)}) copy-start(bf16[384,4096]{1,0:T(8,128)(2,1)} %get-tuple-element.8) | copy-start | bytes 9437188
  225.0 3.2 %copy-start.2 = (bf16[384,4096]{1,0:T(8,128)(2,1)S(1)}, bf16[384,4096]{1,0:T(8,128)(2,1)}, u32[]{:S(2)}) copy-start(bf16[384,4096]{1,0:T(8,128)(2,1)} %get-tuple-element.9) | copy-start | bytes 9437188
  228.1 1.3 copy-start.5
Sparse Core Ops, SparseCore 0:
  9.0 49.0 all-gather.1

commit v3 on v0

v3 whole, which is shorter than its diff:
```python
import functools

import jax
import jax.numpy as jnp
from jax import lax
from jax.experimental import pallas as pl
from jax.experimental.pallas import tpu as pltpu
from jax.sharding import PartitionSpec as P

MESH = pl.DeviceIdType.MESH
WIDTH = 4096
TOKENS = 128
RANK = 64
CHUNKS = 16
COLS = WIDTH // CHUNKS
PAIRS = CHUNKS // 2
SHARE = 128
MAIN = 384
REST = 128
LAG_FORWARD, LAG_ROW, LAG_ROW_FORWARD, LAG_LAST, LAG_USE = 1, 2, 3, 4, 5
LAG_GRAD = 6
SLICE = 32
Q_LAG = 6


def silu_slope(values):
    logistic = jax.nn.sigmoid(values)
    return logistic * (1.0 + values * (1.0 - logistic))


def low_half(shape):
    return lax.broadcasted_iota(jnp.int32, shape, len(shape) - 1) < RANK


def damped_inverses(pair):
    rows = lax.broadcasted_iota(jnp.int32, pair.shape, 0)
    lanes = lax.broadcasted_iota(jnp.int32, pair.shape, 1)
    lower = lanes < RANK
    column = jnp.where(lower, lanes, lanes - RANK)
    diagonal = rows == column
    on_diagonal = jnp.where(diagonal, pair, 0.0)
    trace_first = jnp.sum(jnp.where(lower, on_diagonal, 0.0), keepdims=True)
    trace_second = jnp.sum(jnp.where(lower, 0.0, on_diagonal), keepdims=True)
    damping = jnp.where(lower, trace_first, trace_second) * (0.1 / RANK)
    value = jnp.where(diagonal, pair + damping, pair)
    for k in range(RANK):
        left = jnp.where(
            lower,
            jnp.broadcast_to(value[:, k:k + 1], pair.shape),
            jnp.broadcast_to(value[:, RANK + k:RANK + k + 1], pair.shape),
        )
        pivot = 1.0 / left[k:k + 1]
        row = jnp.where(column[k:k + 1] == k, pivot, value[k:k + 1] * pivot)
        left = jnp.where(rows == k, -1.0, left)
        value = jnp.where((rows == k) | (column == k), 0.0, value) - left * row
    return value


def whole_kernel(
    pool_in, val_in, pool_top, val_top, weight, proj_in, proj_out, valid, counts,
    scores_out,
    held, first, second, gated, grad, total, block, raw, wide_in, wide_out, folded,
    low_mid, low_two, low_in, outgoing,
    landed, factors, factors_z, vals, layers,
    send, recv, grad_send, grad_recv, act_send, act_recv, local, fold_send, fold_recv, proj_send, proj_recv,
    low_send, low_recv, fac_send, fac_recv, val_send, val_recv, facz_send, facz_recv, valz_send, valz_recv,
    lay_send, lay_recv,
):
    layer = lax.axis_index("layer")
    trace = lax.axis_index("trace")
    x, z, c = trace // 8, (trace // 2) % 4, trace % 2
    xp, xm, xo = (x + 1) % 4, (x + 3) % 4, (x + 2) % 4
    zp, zm, zo = (z + 1) % 4, (z + 3) % 4, (z + 2) % 4
    other = 1 - c
    highest = lax.Precision.HIGHEST
    f32, bf16 = jnp.float32, jnp.bfloat16

    def at(xi, zi, ci):
        return {"trace": xi * 8 + zi * 2 + ci}

    above = {"layer": (layer + 1) % 4}
    below = {"layer": (layer + 3) % 4}
    sibling = at(x, z, other)

    near = []
    for dx in range(4):
        for dc in range(2):
            if dx or dc:
                xi, ci = (x + dx) % 4, (c + dc) % 2
                near.append((xi * 2 + ci, xi, ci, at(xi, z, ci)))
    across = [((z + dz) % 4, at(x, (z + dz) % 4, c)) for dz in (1, 3, 2)]
    planes = [((layer + dl) % 4, {"layer": (layer + dl) % 4}) for dl in (1, 3, 2)]
    barrier = pltpu.get_barrier_semaphore()
    for device in [n[3] for n in near] + [a[1] for a in across] + [q[1] for q in planes]:
        pl.semaphore_signal(barrier, inc=1, device_id=device, device_id_type=MESH)
    pl.semaphore_wait(barrier, len(near) + len(across) + len(planes))

    def copy(src, dst, send_sem, recv_sem, device):
        return pltpu.make_async_remote_copy(
            src_ref=src, dst_ref=dst, send_sem=send_sem, recv_sem=recv_sem, device_id=device, device_id_type=MESH
        )

    def columns(j):
        return pl.ds(pl.multiple_of(j * COLS, COLS), COLS)

    def transposed(left, right):
        return lax.dot_general(left, right, (((1,), (1,)), ((), ())), preferred_element_type=f32)

    def on(kind):
        return pl.when(layer == kind)

    def own(j):
        return held.at[j, x, z, c]

    def share_out(j, device):
        return copy(weight.at[:, columns(j)], own(j), send.at[j, 12], recv.at[j, 12], device)

    def share_local(j):
        return pltpu.make_async_copy(weight.at[:, columns(j)], own(j), local.at[j])

    def load(src, dst, index):
        return pltpu.make_async_copy(src, dst, local.at[CHUNKS + index])

    def row_loads(pool, val, target, base):
        return [
            load(pool.at[0], target.at[0:128], base), load(pool.at[1], target.at[128:256], base + 1),
            load(val.at[0], target.at[256:384], base + 2),
        ]

    def loads(kind):
        return {
            3: lambda: row_loads(pool_in, val_in, first, 0) + row_loads(pool_top, val_top, second, 3),
            2: lambda: row_loads(pool_in, val_in, first, 0),
            1: lambda: [load(val_in.at[1], second.at[0:128], 0)],
            0: lambda: [load(val_top.at[1], second.at[0:128], 0)],
        }[kind]()

    def rows_of(base, i):
        return pl.ds(pl.multiple_of(base + i * SLICE, SLICE), SLICE)

    def rest_slice(i, device):
        return copy(
            val_in.at[1, rows_of(0, i)], first.at[rows_of(0, i)], act_send.at[i], act_recv.at[i], device
        )

    def main_slice(i, source, base):
        return copy(
            source.at[rows_of(0, i)], second.at[rows_of(base, i)],
            act_send.at[base // SLICE + i], act_recv.at[base // SLICE + i], above,
        )

    main_sources = ((pool_in.at[0], 0), (pool_in.at[1], 128), (val_in.at[0], 256))

    def gather_stages(j, view, flip, sems, part):
        send_j, recv_j = sems
        ahead, behind, far = (zp, zm, zo) if flip else (xp, xm, xo)
        up, down, beyond = (xp, xm, xo) if flip else (zp, zm, zo)
        lo, mid, hi = part

        def spot(along, over, ci, rows):
            return view(over, along, ci, *rows) if flip else view(along, over, ci, *rows)

        me_along, me_over = (z, x) if flip else (x, z)

        def to_along(i):
            return at(x, i, c) if flip else at(i, z, c)

        def to_over(i):
            return at(i, z, c) if flip else at(x, i, c)

        full = (lo, hi)
        every = slice(0, 4)

        def push(ref, slot, device):
            copy(ref, ref, send_j(j, slot), recv_j(j, slot), device).start()

        def arrived(ref, slot):
            copy(ref, ref, send_j(j, slot), recv_j(j, slot), sibling).wait_recv()

        def share():
            ref = spot(me_along, me_over, c, full)
            push(ref, 0, to_along(ahead))
            push(ref, 1, to_along(behind))

        def forward():
            arrived(spot(behind, me_over, c, full), 0)
            push(spot(behind, me_over, c, (lo, mid)), 2, to_along(ahead))
            arrived(spot(ahead, me_over, c, full), 1)
            push(spot(ahead, me_over, c, (mid, hi)), 3, to_along(behind))

        def row():
            arrived(spot(far, me_over, c, (lo, mid)), 2)
            arrived(spot(far, me_over, c, (mid, hi)), 3)
            ref = spot(every, me_over, c, full)
            push(ref, 4, to_over(up))
            push(ref, 5, to_over(down))
            push(ref, 8, sibling)

        def row_forward():
            arrived(spot(every, down, c, full), 4)
            push(spot(slice(0, 2), down, c, full), 6, to_over(up))
            arrived(spot(every, up, c, full), 5)
            push(spot(slice(2, 4), up, c, full), 7, to_over(down))
            push(spot(every, down, c, full), 9, sibling)
            push(spot(every, up, c, full), 10, sibling)

        def last():
            arrived(spot(slice(0, 2), beyond, c, full), 6)
            arrived(spot(slice(2, 4), beyond, c, full), 7)
            push(spot(every, beyond, c, full), 11, sibling)

        def whole():
            for slot, over in ((8, me_over), (9, down), (10, up), (11, beyond)):
                arrived(spot(every, over, other, full), slot)

        def drain():
            def left(ref, slot):
                copy(ref, ref, send_j(j, slot), recv_j(j, slot), sibling).wait_send()

            for slot in (0, 1):
                left(spot(me_along, me_over, c, full), slot)
            left(spot(me_along, me_over, c, (lo, mid)), 2)
            left(spot(me_along, me_over, c, (mid, hi)), 3)
            for slot in (4, 5, 8, 9, 10, 11):
                left(spot(every, me_over, c, full), slot)
            left(spot(slice(0, 2), me_over, c, full), 6)
            left(spot(slice(2, 4), me_over, c, full), 7)

        return share, forward, row, row_forward, last, whole, drain

    def weight_view(j):
        return lambda xi, zi, ci, lo, hi: held.at[j, xi, zi, ci, lo:hi]

    weight_sems = (lambda j, slot: send.at[j, slot], lambda j, slot: recv.at[j, slot])
    fold_sems = (lambda j, slot: fold_send.at[slot], lambda j, slot: fold_recv.at[slot])

    def weight_stages(p):
        a, b = 2 * p, 2 * p + 1
        part = (0, SHARE // 2, SHARE)
        return zip(
            gather_stages(a, weight_view(a), False, weight_sems, part),
            gather_stages(b, weight_view(b), True, weight_sems, part),
        )

    def run_stage(index):
        def stage(p):
            one, two = list(weight_stages(p))[index]
            one()
            two()
        return stage

    def fold_view(xi, zi, ci, lo, hi):
        return folded.at[xi, zi, ci, lo:hi]

    fold_stages = gather_stages(0, fold_view, False, fold_sems, (RANK, RANK + RANK // 2, 2 * RANK))

    def have_share(p):
        for j in (2 * p, 2 * p + 1):
            @pl.when(layer >= 2)
            def _():
                share_local(j).wait()

            @pl.when(layer < 2)
            def _():
                copy(own(j), own(j), send.at[j, 12], recv.at[j, 12], sibling).wait_recv()

    def half_of(which, index, low, ci):
        return which.at[index, low:low + RANK, pl.ds(pl.multiple_of(ci * (WIDTH // 2), WIDTH // 2), WIDTH // 2)]

    def proj_copy(index, low, slot, device):
        ref = half_of(wide_out, index, low, c)
        return copy(ref, ref, proj_send.at[slot], proj_recv.at[slot], device)

    def proj_out_copies(kind):
        if kind == 2:
            return [proj_copy(1, 0, 3, {"layer": 1})]
        if kind == 1:
            return [proj_copy(0, 0, 0, {"layer": 2})]
        if kind == 0:
            return [proj_copy(0, RANK, 1, {"layer": 1}), proj_copy(0, RANK, 2, {"layer": 2})]
        return []

    def proj_in_copies(kind):
        if kind == 2:
            return [proj_copy(0, 0, 0, above), proj_copy(0, RANK, 2, above)]
        if kind == 1:
            return [proj_copy(0, RANK, 1, above), proj_copy(1, 0, 3, above)]
        return []

    def proj_chip_copies(kind):
        if kind == 2:
            return [proj_copy(0, 0, 4, sibling), proj_copy(0, RANK, 5, sibling)]
        if kind == 1:
            return [proj_copy(0, RANK, 5, sibling), proj_copy(1, 0, 6, sibling)]
        return []

    def proj_chip_arrived(kind):
        for index, low, slot in {2: ((0, 0, 4), (0, RANK, 5)), 1: ((0, RANK, 5), (1, 0, 6))}[kind]:
            ref = half_of(wide_out, index, low, other)
            copy(ref, ref, proj_send.at[slot], proj_recv.at[slot], sibling).wait_recv()

    def turn(store):
        rows = lax.broadcasted_iota(jnp.int32, (2 * RANK, RANK), 0)
        lanes = lax.broadcasted_iota(jnp.int32, (2 * RANK, RANK), 1)
        unit = ((rows % RANK) == lanes).astype(bf16)

        def body(k, carry):
            piece = raw[pl.ds(pl.multiple_of(k * COLS, COLS), COLS), :]
            store(columns(k), transposed(unit, piece).astype(bf16))
            return carry
        lax.fori_loop(0, CHUNKS, body, 0)

    def load_raw(ref):
        return load(ref, raw, 6)

    def block_source(index):
        return (pool_in.at[0], pool_in.at[1], val_in.at[0], val_in.at[1],
                pool_top.at[0], pool_top.at[1], val_top.at[0], val_top.at[1])[index]

    def block_load(source):
        return load(source, block, 7)

    @pl.when(layer >= 2)
    def _():
        def body(j, carry):
            share_local(j).start()
            return carry
        lax.fori_loop(0, CHUNKS, body, 0)

    def share_pair(p):
        for kind, partner in ((3, above), (2, below)):
            @on(kind)
            def _():
                share_out(2 * p, partner).start()
                share_out(2 * p + 1, partner).start()

    share_pair(0)
    share_pair(1)
    load_raw(proj_out).start()
    for kind in range(4):
        @on(kind)
        def _():
            for item in loads(kind):
                item.start()
    block_load(block_source(0)).start()

    def gate_rows(index):
        base = pl.multiple_of(index * 32, 32)
        value = first[pl.ds(base, 32), :].astype(f32)
        top = second[pl.ds(base, 32), :].astype(f32)
        gated[pl.ds(base, 32), :] = (top * silu_slope(value)).astype(bf16)

    def gate_some(start, count):
        def body(i, carry):
            gate_rows(start + i)
            return carry
        lax.fori_loop(0, count, body, 0)

    def grad_copy(j, rows, device):
        return copy(grad.at[j, 0:rows], grad.at[j, 0:rows], grad_send.at[j], grad_recv.at[j], device)

    def upper_chunk(j, rows, device):
        total[0, 0:rows] = second[0:rows, columns(j)].astype(f32)

        def body(xi, carry):
            piece = held[j, xi].reshape(WIDTH // 4, COLS)
            left = gated[0:rows, pl.ds(pl.multiple_of(xi * (WIDTH // 4), WIDTH // 4), WIDTH // 4)]
            total[0, 0:rows] += jnp.dot(left, piece, preferred_element_type=f32)
            return carry
        lax.fori_loop(0, 4, body, 0)
        grad[j, 0:rows] = total[0, 0:rows].astype(bf16)
        grad_copy(j, rows, device).start()

    def add_product(n, q, rows):
        piece = held[n, q // 2, pl.ds(2 * (q % 2), 2)].reshape(4 * SHARE, COLS)
        left = gated[0:rows, pl.ds(pl.multiple_of(q * 2 * COLS, 2 * COLS), 2 * COLS)]
        total[n, 0:rows] += jnp.dot(left, piece, preferred_element_type=f32)

    def lower_weight(n, ready, rows):
        total[n, 0:rows] = jnp.zeros((rows, COLS), f32)

        def body(q, carry):
            add_product(n, q, rows)
            return carry
        lax.fori_loop(0, ready, body, 0)

    def lower_gate(q, rows):
        for k in (2 * q, 2 * q + 1):
            grad_copy(k, rows, above).wait_recv()

            def gating(i, carry):
                base = pl.multiple_of(i * 64, 64)
                value = first[pl.ds(base, 64), columns(k)].astype(f32)
                up = grad[k, pl.ds(base, 64)].astype(f32)
                gated[pl.ds(base, 64), columns(k)] = (up * silu_slope(value)).astype(bf16)
                return carry
            lax.fori_loop(0, rows // 64, gating, 0)

    def lower_grad(q, ready, rows):
        lower_gate(q, rows)

        def body(n, carry):
            add_product(n, q, rows)
            return carry
        lax.fori_loop(0, ready, body, 0)

    def when_in(t, lag, what):
        @pl.when((t >= lag) & (t < PAIRS + lag))
        def _():
            what(t - lag)

    def early(t):
        @pl.when(t == 0)
        def _():
            load_raw(proj_out).wait()

            def keep_out(cols, value):
                @pl.when(layer >= 2)
                def _():
                    wide_out[1, :, cols] = value

                @on(1)
                def _():
                    wide_out[0, 0:RANK, cols] = value[0:RANK]

                @on(0)
                def _():
                    wide_out[0, RANK:2 * RANK, cols] = value[0:RANK]
            turn(keep_out)
            for kind in (2, 1, 0):
                @on(kind)
                def _():
                    for item in proj_out_copies(kind):
                        item.start()
            load_raw(proj_in).start()
            folded[:, :, :, 0:RANK] = jnp.zeros((4, 4, 2, RANK, 2 * RANK), bf16)

        @pl.when(t == 1)
        def _():
            load_raw(proj_in).wait()

            def keep_in(cols, value):
                wide_in[:, cols] = value
            turn(keep_in)
            for kind in range(4):
                @on(kind)
                def _():
                    for item in loads(kind):
                        item.wait()

        for index in range(4):
            @pl.when(t == 1 + index)
            def _():
                block_load(block_source(index)).wait()
                low_in[index] = transposed(block[...], wide_in[...])
                if index < 3:
                    block_load(block_source(index + 1)).start()
                else:
                    @on(3)
                    def _():
                        block_load(block_source(4)).start()

                    @on(1)
                    def _():
                        block_load(weight).start()
        for index in range(4, 8):
            @pl.when((t == 1 + index) & (layer == 3))
            def _():
                block_load(block_source(index)).wait()
                low_mid[pl.ds((index - 4) * TOKENS, TOKENS)] = transposed(block[...], wide_out[1])
                if index < 7:
                    block_load(block_source(index + 1)).start()

        @pl.when((t >= 1) & (t < 5) & (layer == 3))
        def _():
            gate_some(3 * (t - 1), 3)

        for kind in (2, 1):
            @pl.when((t == 3) & (layer == kind))
            def _():
                for item in proj_in_copies(kind):
                    item.wait_recv()
                for item in proj_chip_copies(kind):
                    item.start()

            @pl.when((t == 4) & (layer == kind))
            def _():
                proj_chip_arrived(kind)
                if kind == 1:
                    wide_out[1, RANK:2 * RANK] = wide_out[1, 0:RANK]

        @pl.when((t == 5) & (layer == 1))
        def _():
            block_load(weight).wait()
            folded[x, z, c, RANK:2 * RANK] = transposed(wide_out[0, RANK:2 * RANK], block[...]).astype(bf16)
            mine = folded.at[x, z, c, RANK:2 * RANK]
            copy(mine, mine, fold_send.at[12], fold_recv.at[12], above).start()

        for index, stage in enumerate(fold_stages[:6]):
            @pl.when((t == Q_LAG + index) & ((layer == 1) | (layer == 2)))
            def _():
                if index == 0:
                    @on(2)
                    def _():
                        mine = folded.at[x, z, c, RANK:2 * RANK]
                        copy(mine, mine, fold_send.at[12], fold_recv.at[12], above).wait_recv()
                stage()

    def step(t, carry):
        @pl.when(t + 2 < PAIRS)
        def _():
            share_pair(t + 2)
        for kind, partner in ((3, above), (2, below)):
            @pl.when((t < 4) & (layer == kind))
            def _():
                rest_slice(t, partner).start()

        @pl.when((t < 4) & (layer == 1))
        def _():
            for source, base in main_sources:
                main_slice(t, source, base).start()

        when_in(t, 0, have_share)
        for lag, index in ((0, 0), (LAG_FORWARD, 1), (LAG_ROW, 2), (LAG_ROW_FORWARD, 3), (LAG_LAST, 4)):
            when_in(t, lag, run_stage(index))
        early(t)
        when_in(t, LAG_USE, run_stage(5))

        @pl.when((t == LAG_USE) & (layer < 2))
        def _():
            for i in range(4):
                rest_slice(i, above).wait_recv()

            @on(0)
            def _():
                gate_some(0, REST // 32)

        for kind, rows, target in ((3, MAIN, below), (0, REST, above)):
            @pl.when((layer == kind) & (t >= LAG_USE) & (t < PAIRS + LAG_USE))
            def _():
                upper_chunk(2 * (t - LAG_USE), rows, target)
                upper_chunk(2 * (t - LAG_USE) + 1, rows, target)

        whole = jnp.minimum(2 * (t - LAG_USE) + 2, CHUNKS)
        for kind, rows in ((2, MAIN), (1, REST)):
            @pl.when((layer == kind) & (t >= LAG_USE) & (t < PAIRS + LAG_USE))
            def _():
                ready = jnp.maximum(t - LAG_GRAD, 0)
                lower_weight(2 * (t - LAG_USE), ready, rows)
                lower_weight(2 * (t - LAG_USE) + 1, ready, rows)

            @pl.when((layer == kind) & (t >= LAG_GRAD) & (t < PAIRS + LAG_GRAD - 1))
            def _():
                lower_grad(t - LAG_GRAD, whole, rows)
        return carry

    lax.fori_loop(0, PAIRS + LAG_GRAD - 1, step, 0)

    def finish(kind, rows):
        if kind == 2:
            for i in range(4):
                for source, base in main_sources:
                    main_slice(i, source, base).wait_recv()
        lower_gate(PAIRS - 1, rows)
        low_mid[0:rows] = jnp.zeros((rows, 2 * RANK), f32)
        low_two[0:rows] = jnp.zeros((rows, 2 * RANK), f32)

        def body(n, carry):
            add_product(n, PAIRS - 1, rows)
            low_two[0:rows] += transposed(grad[n, 0:rows], wide_out[1, :, columns(n)])

            def inner(i, inner_carry):
                base = pl.multiple_of(i * 64, 64)
                up = grad[n, pl.ds(base, 64)].astype(f32)
                value = second[pl.ds(base, 64), columns(n)].astype(f32)
                low = (up + total[n, pl.ds(base, 64)]).astype(bf16)
                first[pl.ds(base, 64), columns(n)] = low
                grad[n, pl.ds(base, 64)] = (low.astype(f32) * silu_slope(value)).astype(bf16)
                return inner_carry
            lax.fori_loop(0, rows // 64, inner, 0)
            fold = folded[n // 4, n % 4]
            low_mid[0:rows] += (
                transposed(first[0:rows, columns(n)], wide_out[0, :, columns(n)])
                + transposed(grad[n, 0:rows, 0:SHARE], fold[0])
                + transposed(grad[n, 0:rows, SHARE:COLS], fold[1])
            )
            return carry
        lax.fori_loop(0, CHUNKS, body, 0)

    wide = (RANK, 2 * RANK)
    lower = low_half(wide)
    lower_rows = low_half((TOKENS, 2 * RANK))

    def swap(value):
        return pltpu.roll(value, RANK, 1)

    def put(index, slot, value, mask):
        outgoing[index, slot] = (value * valid[mask]).astype(bf16)

    @on(3)
    def _():
        rows = [low_mid[i * TOKENS:(i + 1) * TOKENS] for i in range(4)]
        landed[0] = (jnp.where(lower_rows, rows[0], rows[1]) * valid[0]).astype(bf16)
        landed[1] = (jnp.where(lower_rows, rows[2], rows[3]) * valid[1]).astype(bf16)
        landed[2] = jnp.zeros_like(landed[2])

    @on(2)
    def _():
        finish(2, MAIN)
        mid = [low_mid[i * TOKENS:(i + 1) * TOKENS] for i in range(3)]
        two = [low_two[i * TOKENS:(i + 1) * TOKENS] for i in range(3)]
        put(1, 0, jnp.where(lower_rows, mid[0], swap(mid[1])), 0)
        put(1, 1, jnp.where(lower_rows, mid[2], 0.0), 1)
        put(0, 0, jnp.where(lower_rows, swap(mid[0]), mid[1]), 0)
        put(0, 1, jnp.where(lower_rows, swap(mid[2]), 0.0), 1)
        landed[0] = (jnp.where(lower_rows, two[0], two[1]) * valid[0]).astype(bf16)
        landed[1] = (jnp.where(lower_rows, two[2], 0.0) * valid[1]).astype(bf16)

    @on(1)
    def _():
        finish(1, REST)
        mid, two = low_mid[0:TOKENS], low_two[0:TOKENS]
        put(0, 1, jnp.where(lower_rows, 0.0, mid), 1)
        put(2, 1, jnp.where(lower_rows, 0.0, two), 1)
        landed[2] = (jnp.where(lower_rows, 0.0, swap(mid)) * valid[1]).astype(bf16)

    def low(source, slot, plane):
        return copy(source, landed.at[slot], low_send.at[slot + 3 * plane], low_recv.at[slot], {"layer": plane})

    def lows(kind):
        if kind == 2:
            return [low(outgoing.at[1, 0], 0, 1), low(outgoing.at[1, 1], 1, 1),
                    low(outgoing.at[0, 0], 0, 0), low(outgoing.at[0, 1], 1, 0)]
        if kind == 1:
            return [low(outgoing.at[0, 1], 2, 0), low(outgoing.at[2, 1], 2, 2)]
        return []

    def lows_in(kind):
        return [low(landed.at[slot], slot, (kind + 1) % 4) for slot in {3: (), 2: (2,), 1: (0, 1), 0: (0, 1, 2)}[kind]]

    for kind in (2, 1):
        @pl.when(layer == kind)
        def _():
            for item in lows(kind):
                item.start()

    for kind in (2, 1, 0):
        @pl.when(layer == kind)
        def _():
            for item in lows_in(kind):
                item.wait_recv()

    def across_tokens(left, right):
        return lax.dot_general(left, right, (((0,), (0,)), ((), ())), precision=highest, preferred_element_type=f32)

    def blocks(value):
        return jnp.where(lower, value[0:RANK], value[RANK:2 * RANK])

    def both(value):
        return value + swap(value)

    pool_low = jnp.where(lower_rows, low_in[0], low_in[1]) * valid[0]
    val_low = jnp.where(lower_rows, low_in[2], low_in[3]) * valid[1]
    pool_out = landed[0].astype(f32)
    val_out = landed[1].astype(f32) + landed[2].astype(f32)
    vals[x, z, c] = blocks(across_tokens(val_out, val_low)).astype(bf16)
    part_in = both(blocks(across_tokens(pool_low, pool_low)))
    part_out = both(blocks(across_tokens(pool_out, pool_out)))
    factors[x * 2 + c, 0:RANK] = jnp.where(lower, part_in, part_out)
    factors[x * 2 + c, RANK:RANK + 8] = counts[...]

    mine = x * 2 + c
    sent_one = [copy(factors.at[mine], factors.at[mine], fac_send.at[i], fac_recv.at[mine], n[3]) for i, n in enumerate(near)]
    sent_one += [copy(vals.at[x, z, c], vals.at[x, z, c], val_send.at[i], val_recv.at[mine], n[3]) for i, n in enumerate(near)]
    for item in sent_one:
        item.start()
    pool_grads = blocks(across_tokens(pool_low, pool_out))
    for slot, xi, ci, device in near:
        copy(factors.at[slot], factors.at[slot], fac_send.at[0], fac_recv.at[slot], device).wait_recv()
    factors_z[z] = sum(factors[i] for i in range(1, 8)) + factors[0]
    sent_two = [copy(factors_z.at[z], factors_z.at[z], facz_send.at[i], facz_recv.at[z], a[1]) for i, a in enumerate(across)]
    for item in sent_two:
        item.start()
    for slot, xi, ci, device in near:
        copy(vals.at[xi, z, ci], vals.at[xi, z, ci], val_send.at[0], val_recv.at[slot], device).wait_recv()
    sent_three = [copy(vals.at[:, z], vals.at[:, z], valz_send.at[i], valz_recv.at[z], a[1]) for i, a in enumerate(across)]
    for item in sent_three:
        item.start()
    for zi, device in across:
        copy(factors_z.at[zi], factors_z.at[zi], facz_send.at[0], facz_recv.at[zi], device).wait_recv()
    factor_sum = factors_z[0] + factors_z[1] + factors_z[2] + factors_z[3]
    inverse = damped_inverses(factor_sum[0:RANK] / factor_sum[RANK:RANK + 1])
    inv_in = inverse[:, 0:RANK]
    turned = swap(inverse)
    twice = jnp.where(lower, turned, inverse)
    inv_out = jnp.concatenate([jnp.where(lower, twice, 0.0), jnp.where(lower, 0.0, twice)], 0)
    scaled = jnp.dot(inv_in, pool_grads, precision=highest, preferred_element_type=f32)
    scaled = jnp.dot(scaled, inv_out, precision=highest, preferred_element_type=f32)
    coarse = scaled.astype(bf16)
    fine = (scaled - coarse.astype(f32)).astype(bf16)
    empty = jnp.zeros(wide, bf16)

    def spread(value):
        return jnp.concatenate(
            [jnp.concatenate([value, empty], 1), jnp.concatenate([empty, value], 1)], 0
        )

    coarse, fine = spread(coarse), spread(fine)
    for zi, device in across:
        copy(vals.at[:, zi], vals.at[:, zi], valz_send.at[0], valz_recv.at[zi], device).wait_recv()
    every = vals[...].reshape(32 * RANK, 2 * RANK)
    product = jnp.dot(every, coarse, preferred_element_type=f32) + jnp.dot(every, fine, preferred_element_type=f32)
    at_row = lax.broadcasted_iota(jnp.int32, product.shape, 0) % RANK
    at_lane = lax.broadcasted_iota(jnp.int32, product.shape, 1) % RANK
    summed = jnp.where(at_row == at_lane, product, 0.0).reshape(32, RANK, 4 * RANK).sum(1)
    group = lax.broadcasted_iota(jnp.int32, (8, 4 * RANK), 1) // RANK
    picks = (lax.broadcasted_iota(jnp.int32, (8, 4 * RANK), 0) == group).astype(f32)
    part = lax.dot_general(picks, summed, (((1,), (1,)), ((), ())), precision=highest, preferred_element_type=f32)
    layers[layer] = jnp.concatenate([part, jnp.zeros((8, 96), f32)], 1)
    sent_last = [copy(layers.at[layer], layers.at[layer], lay_send.at[i], lay_recv.at[layer], q[1]) for i, q in enumerate(planes)]
    for item in sent_last:
        item.start()
    for plane, device in planes:
        copy(layers.at[plane], layers.at[plane], lay_send.at[0], lay_recv.at[plane], device).wait_recv()
    scores_out[...] = (layers[0] + layers[1] + layers[2] + layers[3]) * (1.0 / (RANK * TOKENS))

    for item in sent_one + sent_two + sent_three + sent_last:
        item.wait_send()
    for kind in (2, 1):
        @pl.when(layer == kind)
        def _():
            for item in lows(kind):
                item.wait_send()

    def drain(p, carry):
        run_stage(6)(p)

        @pl.when(layer >= 2)
        def _():
            share_out(2 * p, above).wait_send()
            share_out(2 * p + 1, above).wait_send()
        for kind, rows in ((3, MAIN), (0, REST)):
            @on(kind)
            def _():
                grad_copy(2 * p, rows, above).wait_send()
                grad_copy(2 * p + 1, rows, above).wait_send()
        return carry
    lax.fori_loop(0, PAIRS, drain, 0)

    @pl.when(layer >= 2)
    def _():
        for i in range(4):
            rest_slice(i, above).wait_send()

    @on(1)
    def _():
        for i in range(4):
            for source, base in main_sources:
                main_slice(i, source, base).wait_send()
        mine = folded.at[x, z, c, RANK:2 * RANK]
        copy(mine, mine, fold_send.at[12], fold_recv.at[12], above).wait_send()

    @pl.when((layer == 1) | (layer == 2))
    def _():
        fold_stages[6]()
    for kind in (2, 1, 0):
        @on(kind)
        def _():
            for item in proj_out_copies(kind) + proj_chip_copies(kind):
                item.wait_send()


def whole(*operands):
    anywhere = pl.BlockSpec(memory_space=pl.ANY)
    inside = pl.BlockSpec(memory_space=pltpu.VMEM)
    dma = pltpu.SemaphoreType.DMA
    bf16, f32 = jnp.bfloat16, jnp.float32
    return pl.pallas_call(
        whole_kernel,
        out_shape=jax.ShapeDtypeStruct((8, 128), f32),
        in_specs=[anywhere] * 7 + [inside] * 2,
        out_specs=inside,
        scratch_shapes=[
            pltpu.VMEM((CHUNKS, 4, 4, 2, SHARE, COLS), bf16),
            pltpu.VMEM((MAIN, WIDTH), bf16),
            pltpu.VMEM((MAIN, WIDTH), bf16),
            pltpu.VMEM((MAIN, WIDTH), bf16),
            pltpu.VMEM((CHUNKS, MAIN, COLS), bf16),
            pltpu.VMEM((CHUNKS, MAIN, COLS), f32),
            pltpu.VMEM((TOKENS, WIDTH), bf16),
            pltpu.VMEM((WIDTH, RANK), bf16),
            pltpu.VMEM((2 * RANK, WIDTH), bf16),
            pltpu.VMEM((2, 2 * RANK, WIDTH), bf16),
            pltpu.VMEM((4, 4, 2, 2 * RANK, SHARE), bf16),
            pltpu.VMEM((4 * TOKENS, 2 * RANK), f32),
            pltpu.VMEM((MAIN, 2 * RANK), f32),
            pltpu.VMEM((4, TOKENS, 2 * RANK), f32),
            pltpu.VMEM((3, 2, TOKENS, 2 * RANK), bf16),
            pltpu.VMEM((3, TOKENS, 2 * RANK), bf16),
            pltpu.VMEM((8, RANK + 8, 2 * RANK), f32),
            pltpu.VMEM((4, RANK + 8, 2 * RANK), f32),
            pltpu.VMEM((4, 4, 2, RANK, 2 * RANK), bf16),
            pltpu.VMEM((4, 8, 128), f32),
            dma((CHUNKS, 13)), dma((CHUNKS, 13)), dma((CHUNKS,)), dma((CHUNKS,)), dma((12,)), dma((12,)),
            dma((CHUNKS + 8,)), dma((13,)), dma((13,)), dma((7,)), dma((7,)),
            dma((12,)), dma((3,)), dma((7,)), dma((8,)), dma((7,)), dma((8,)),
            dma((3,)), dma((4,)), dma((3,)), dma((4,)), dma((3,)), dma((4,)),
        ],
        compiler_params=pltpu.CompilerParams(
            collective_id=0, has_side_effects=True, vmem_limit_bytes=62 * 1024 * 1024
        ),
        name="whole",
    )(*operands)


def on_device(
    pool_inputs, val_inputs, pool_top, val_top, weight, proj_in, proj_out, pool_len, val_len
):
    layer = lax.axis_index("layer")
    positions = jnp.arange(TOKENS, dtype=jnp.int32)
    lengths = jnp.stack([pool_len, val_len])
    valid = (positions[None, :, None] < lengths[:, None, :]).astype(jnp.float32)
    valid = jnp.repeat(valid, RANK, axis=2)
    counts = jnp.full((8, 2 * RANK), jnp.sum(pool_len).astype(jnp.float32))
    summed = whole(
        pool_inputs[0], val_inputs[0], pool_top, val_top, weight[0], proj_in[0], proj_out[0], valid, counts
    )
    table = summed[:4, :32].reshape(2, 2, 32).transpose(1, 2, 0).reshape(2, 64)
    return lax.dynamic_slice_in_dim(table, layer * 16, 16, 1)


def solution(mesh):
    placed = (
        P("layer", "trace", None, None),
        P("layer", "trace", None, None),
        P("trace", None, None),
        P("trace", None, None),
        P("layer", "trace", None),
        P("layer", None, None),
        P("layer", None, None),
        P("trace"),
        P("trace"),
    )
    return jax.shard_map(
        on_device, mesh=mesh, in_specs=placed, out_specs=P("trace", "layer"), check_vma=False
    )
```

time: 851 us -> 198 us (0.23)
  waiting for transfers between devices: 585 us -> 0 us
  Pallas kernels: 0 us -> 189 us
  blocking collectives: 125 us -> 0 us
  other arithmetic: 58.1 us -> 2.11 us
  matrix products: 42.3 us -> 0 us
  between operations: 15.3 us -> 0.67 us
  starting transfers between devices: 9.06 us -> 0 us
    ppermute x4 -> x0, waiting for transfers between devices: 422 us -> none  [passed_along(): lax.ppermute(value, axis, [(source, source + steps) for source in range(f...]
    pallas_call x0 -> x1, Pallas kernels: none -> 189 us  [whole(): pl.pallas_call(whole_kernel, out_shape=jax.ShapeDtypeStruct((8, 128), f32...]
    all_gather x2 -> x0, waiting for transfers between devices: 145 us -> none  [the longest x1 107 us: on_device(): full_weight = lax.all_gather(weight[0], 'trace', axis=0, tiled=True)]
    psum x1 -> x0, blocking collectives: 125 us -> none  [on_device(): lax.psum((local_in, local_out, local_count), 'trace')]
    dot_general x8 -> x0, matrix products: 39.9 us -> none  [the longest x1 30.7 us: lower_grad(): jnp.dot(gated, full_weight, preferred_element_type=jnp.float32)]
    another operation x10 -> x1, other arithmetic: 24.2 us -> 0.68 us  [on_device(): lengths = jnp.stack([pool_len, val_len])]
    select_n x4 -> x0, other arithmetic: 22.4 us -> none  [chain_step(): held_grads = jnp.where(active, current, held_grads)]
    unnamed x4 -> x0, waiting for transfers between devices: 18.5 us -> none
  transfers between devices with their start and end apart: 7 -> 0, of which waited for: 7 -> 0; matrix products, arithmetic and copies ran while one was open for 1% -> 0% of each run, Pallas kernels for 0% -> 0%
where the time goes in v3:
time: 198 us
  Pallas kernels  189 us (95%)
  local copies, waits for them, and re-layouts  6.64 us (3%)
  other arithmetic  2.11 us (1%)
    pallas_call x1, Pallas kernels, whole(): pl.pallas_call(whole_kernel, out_shape=jax.ShapeDtypeStruct((8, 128), f32...  189 us

profile of v3, /device:TPU:8, one launch (start us, length us, event | category | flops | bytes accessed | tf_op | source)
XLA Modules:
  0.0 198.2 jit_solution(10264955883352200770)
XLA Ops:
  0.0 0.0 copy-start
  0.0 1.4 reduce_sum.9
  2.0 0.7 pad_add_fusion
  2.7 0.1 compare_convert_fusion
  2.8 0.6 broadcast_in_dim.9.counts
  3.4 0.8 copy.15.valid
  4.1 2.4 %copy.13 = bf16[1,4096,64]{2,1,0:T(8,128)(2,1)} copy(bf16[1,4096,64]{1,2,0:T(8,128)(2,1)} %param.14) | data formatting | bytes 1048576 | tf_op args[5]
  6.5 0.0 copy-done
  6.5 1.4 copy.14
  7.9 188.7 %whole.1 = f32[8,128]{1,0:T(8,128)} custom-call(bf16[2,128,4096]{2,1,0:T(8,128)(2,1)} %bitcast.13, bf16[2,128,4096]{2,1,0:T(8,128)(2,1)} %bitcast.14, bf16[2,128,4096]{2,1,0:T(8,128)(2,1)} %pool_top.1, bf16[2,128,4096]{2,1,0:T(8,128)(2,1)} %val_top.1, bf16[128,4096]{1,0:T(8,128)(2,1)} %bitcast.15, bf16[4096,64]{1,0:T(8,128)(2,1)} %bitcast.11, ...), custom_call_target="tpu_custom_call" | custom-call | tf_op jit(solution)/shard_map/whole/pallas_call | solution.py:778
  196.6 0.7 slice.3
  197.3 0.1 copy.16
  197.4 0.1 reshape.12
  197.5 0.6 constant_dynamic-slice_fusion
  (1 shorter events, 0.0 us)
Async XLA Ops:
  0.0 6.5 %copy-start = (bf16[1,4096,64]{1,2,0:T(8,128)(2,1)S(1)}, bf16[1,4096,64]{1,2,0:T(8,128)(2,1)}, u32[]{:S(2)}) copy-start(bf16[1,4096,64]{1,2,0:T(8,128)(2,1)} %param.15) | copy-start | bytes 1572868

commit v4 on v3

--- a/solution.py
+++ b/solution.py
@@ -20,6 +20,7 @@
 LAG_FORWARD, LAG_ROW, LAG_ROW_FORWARD, LAG_LAST, LAG_USE = 1, 2, 3, 4, 5
 LAG_GRAD = 6
 SLICE = 32
+PART = 16
 Q_LAG = 6
 
 
@@ -57,9 +58,9 @@
 
 
 def whole_kernel(
-    pool_in, val_in, pool_top, val_top, weight, proj_in, proj_out, valid, counts,
+    pool_in, val_in, pool_top, val_top, weight, proj_in, proj_out, pool_len, val_len,
     scores_out,
-    held, first, second, gated, grad, total, block, raw, wide_in, wide_out, folded,
+    held, first, second, gated, grad, total, block, wide_in, wide_out, folded,
     low_mid, low_two, low_in, outgoing,
     landed, factors, factors_z, vals, layers,
     send, recv, grad_send, grad_recv, act_send, act_recv, local, fold_send, fold_recv, proj_send, proj_recv,
@@ -144,10 +145,10 @@
         )
 
     def main_slice(i, source, base):
-        return copy(
-            source.at[rows_of(0, i)], second.at[rows_of(base, i)],
-            act_send.at[base // SLICE + i], act_recv.at[base // SLICE + i], above,
-        )
+        rows = pl.ds(pl.multiple_of(i * PART, PART), PART)
+        there = pl.ds(pl.multiple_of(base + i * PART, PART), PART)
+        index = base // PART + i
+        return copy(source.at[rows], second.at[there], act_send.at[index], act_recv.at[index], above)
 
     main_sources = ((pool_in.at[0], 0), (pool_in.at[1], 128), (val_in.at[0], 256))
 
@@ -299,19 +300,16 @@
             ref = half_of(wide_out, index, low, other)
             copy(ref, ref, proj_send.at[slot], proj_recv.at[slot], sibling).wait_recv()
 
-    def turn(store):
-        rows = lax.broadcasted_iota(jnp.int32, (2 * RANK, RANK), 0)
-        lanes = lax.broadcasted_iota(jnp.int32, (2 * RANK, RANK), 1)
-        unit = ((rows % RANK) == lanes).astype(bf16)
-
-        def body(k, carry):
-            piece = raw[pl.ds(pl.multiple_of(k * COLS, COLS), COLS), :]
-            store(columns(k), transposed(unit, piece).astype(bf16))
-            return carry
-        lax.fori_loop(0, CHUNKS, body, 0)
-
-    def load_raw(ref):
-        return load(ref, raw, 6)
+    def proj_loads(kind):
+        places = {
+            3: [(1, 0), (1, RANK)], 2: [(1, 0), (1, RANK)], 1: [(0, 0)], 0: [(0, RANK)],
+        }[kind]
+        return [
+            load(proj_out, wide_out.at[index, low:low + RANK], 8 + i) for i, (index, low) in enumerate(places)
+        ]
+
+    def proj_in_loads():
+        return [load(proj_in, wide_in.at[i * RANK:(i + 1) * RANK], 10 + i) for i in range(2)]
 
     def block_source(index):
         return (pool_in.at[0], pool_in.at[1], val_in.at[0], val_in.at[1],
@@ -336,12 +334,13 @@
 
     share_pair(0)
     share_pair(1)
-    load_raw(proj_out).start()
     for kind in range(4):
         @on(kind)
         def _():
-            for item in loads(kind):
+            for item in proj_loads(kind) + loads(kind):
                 item.start()
+    for item in proj_in_loads():
+        item.start()
     block_load(block_source(0)).start()
 
     def gate_rows(index):
@@ -378,9 +377,11 @@
 
     def lower_weight(n, ready, rows):
         total[n, 0:rows] = jnp.zeros((rows, COLS), f32)
+        total[n + 1, 0:rows] = jnp.zeros((rows, COLS), f32)
 
         def body(q, carry):
             add_product(n, q, rows)
+            add_product(n + 1, q, rows)
             return carry
         lax.fori_loop(0, ready, body, 0)
 
@@ -400,9 +401,10 @@
         lower_gate(q, rows)
 
         def body(n, carry):
-            add_product(n, q, rows)
+            add_product(2 * n, q, rows)
+            add_product(2 * n + 1, q, rows)
             return carry
-        lax.fori_loop(0, ready, body, 0)
+        lax.fori_loop(0, ready // 2, body, 0)
 
     def when_in(t, lag, what):
         @pl.when((t >= lag) & (t < PAIRS + lag))
@@ -412,36 +414,19 @@
     def early(t):
         @pl.when(t == 0)
         def _():
-            load_raw(proj_out).wait()
-
-            def keep_out(cols, value):
-                @pl.when(layer >= 2)
-                def _():
-                    wide_out[1, :, cols] = value
-
-                @on(1)
-                def _():
-                    wide_out[0, 0:RANK, cols] = value[0:RANK]
-
-                @on(0)
-                def _():
-                    wide_out[0, RANK:2 * RANK, cols] = value[0:RANK]
-            turn(keep_out)
-            for kind in (2, 1, 0):
+            for kind in range(4):
                 @on(kind)
                 def _():
+                    for item in proj_loads(kind):
+                        item.wait()
                     for item in proj_out_copies(kind):
                         item.start()
-            load_raw(proj_in).start()
             folded[:, :, :, 0:RANK] = jnp.zeros((4, 4, 2, RANK, 2 * RANK), bf16)
 
         @pl.when(t == 1)
         def _():
-            load_raw(proj_in).wait()
-
-            def keep_in(cols, value):
-                wide_in[:, cols] = value
-            turn(keep_in)
+            for item in proj_in_loads():
+                item.wait()
             for kind in range(4):
                 @on(kind)
                 def _():
@@ -515,10 +500,10 @@
             def _():
                 rest_slice(t, partner).start()
 
-        @pl.when((t < 4) & (layer == 1))
+        @pl.when((t >= 1) & (t < 9) & (layer == 1))
         def _():
             for source, base in main_sources:
-                main_slice(t, source, base).start()
+                main_slice(t - 1, source, base).start()
 
         when_in(t, 0, have_share)
         for lag, index in ((0, 0), (LAG_FORWARD, 1), (LAG_ROW, 2), (LAG_ROW_FORWARD, 3), (LAG_LAST, 4)):
@@ -547,7 +532,6 @@
             def _():
                 ready = jnp.maximum(t - LAG_GRAD, 0)
                 lower_weight(2 * (t - LAG_USE), ready, rows)
-                lower_weight(2 * (t - LAG_USE) + 1, ready, rows)
 
             @pl.when((layer == kind) & (t >= LAG_GRAD) & (t < PAIRS + LAG_GRAD - 1))
             def _():
@@ -558,7 +542,7 @@
 
     def finish(kind, rows):
         if kind == 2:
-            for i in range(4):
+            for i in range(8):
                 for source, base in main_sources:
                     main_slice(i, source, base).wait_recv()
         lower_gate(PAIRS - 1, rows)
@@ -591,6 +575,11 @@
     lower = low_half(wide)
     lower_rows = low_half((TOKENS, 2 * RANK))
 
+    tokens = lax.broadcasted_iota(jnp.int32, (TOKENS, 2 * RANK), 0)
+    valid = [
+        (tokens < jnp.where(lower_rows, lens[0], lens[1])).astype(f32) for lens in (pool_len, val_len)
+    ]
+
     def swap(value):
         return pltpu.roll(value, RANK, 1)
 
@@ -667,7 +656,7 @@
     part_in = both(blocks(across_tokens(pool_low, pool_low)))
     part_out = both(blocks(across_tokens(pool_out, pool_out)))
     factors[x * 2 + c, 0:RANK] = jnp.where(lower, part_in, part_out)
-    factors[x * 2 + c, RANK:RANK + 8] = counts[...]
+    factors[x * 2 + c, RANK:RANK + 8] = jnp.full((8, 2 * RANK), (pool_len[0] + pool_len[1]).astype(f32))
 
     mine = x * 2 + c
     sent_one = [copy(factors.at[mine], factors.at[mine], fac_send.at[i], fac_recv.at[mine], n[3]) for i, n in enumerate(near)]
@@ -722,7 +711,16 @@
         item.start()
     for plane, device in planes:
         copy(layers.at[plane], layers.at[plane], lay_send.at[0], lay_recv.at[plane], device).wait_recv()
-    scores_out[...] = (layers[0] + layers[1] + layers[2] + layers[3]) * (1.0 / (RANK * TOKENS))
+    table = (layers[0] + layers[1] + layers[2] + layers[3]) * (1.0 / (RANK * TOKENS))
+    lane = lax.broadcasted_iota(jnp.int32, (128, 16), 0)
+    spot_of = lax.broadcasted_iota(jnp.int32, (128, 16), 1) + 16 * layer
+
+    def placed(index):
+        return jnp.dot(
+            table, (2 * lane + index == spot_of).astype(f32), precision=highest, preferred_element_type=f32
+        )
+
+    scores_out[...] = placed(0)[0:2] + placed(1)[2:4]
 
     for item in sent_one + sent_two + sent_three + sent_last:
         item.wait_send()
@@ -754,7 +752,7 @@
 
     @on(1)
     def _():
-        for i in range(4):
+        for i in range(8):
             for source, base in main_sources:
                 main_slice(i, source, base).wait_send()
         mine = folded.at[x, z, c, RANK:2 * RANK]
@@ -777,8 +775,8 @@
     bf16, f32 = jnp.bfloat16, jnp.float32
     return pl.pallas_call(
         whole_kernel,
-        out_shape=jax.ShapeDtypeStruct((8, 128), f32),
-        in_specs=[anywhere] * 7 + [inside] * 2,
+        out_shape=jax.ShapeDtypeStruct((2, 16), f32),
+        in_specs=[anywhere] * 7 + [pl.BlockSpec(memory_space=pltpu.SMEM)] * 2,
         out_specs=inside,
         scratch_shapes=[
             pltpu.VMEM((CHUNKS, 4, 4, 2, SHARE, COLS), bf16),
@@ -788,7 +786,6 @@
             pltpu.VMEM((CHUNKS, MAIN, COLS), bf16),
             pltpu.VMEM((CHUNKS, MAIN, COLS), f32),
             pltpu.VMEM((TOKENS, WIDTH), bf16),
-            pltpu.VMEM((WIDTH, RANK), bf16),
             pltpu.VMEM((2 * RANK, WIDTH), bf16),
             pltpu.VMEM((2, 2 * RANK, WIDTH), bf16),
             pltpu.VMEM((4, 4, 2, 2 * RANK, SHARE), bf16),
@@ -801,8 +798,8 @@
             pltpu.VMEM((4, RANK + 8, 2 * RANK), f32),
             pltpu.VMEM((4, 4, 2, RANK, 2 * RANK), bf16),
             pltpu.VMEM((4, 8, 128), f32),
-            dma((CHUNKS, 13)), dma((CHUNKS, 13)), dma((CHUNKS,)), dma((CHUNKS,)), dma((12,)), dma((12,)),
-            dma((CHUNKS + 8,)), dma((13,)), dma((13,)), dma((7,)), dma((7,)),
+            dma((CHUNKS, 13)), dma((CHUNKS, 13)), dma((CHUNKS,)), dma((CHUNKS,)), dma((24,)), dma((24,)),
+            dma((CHUNKS + 12,)), dma((13,)), dma((13,)), dma((7,)), dma((7,)),
             dma((12,)), dma((3,)), dma((7,)), dma((8,)), dma((7,)), dma((8,)),
             dma((3,)), dma((4,)), dma((3,)), dma((4,)), dma((3,)), dma((4,)),
         ],
@@ -816,17 +813,9 @@
 def on_device(
     pool_inputs, val_inputs, pool_top, val_top, weight, proj_in, proj_out, pool_len, val_len
 ):
-    layer = lax.axis_index("layer")
-    positions = jnp.arange(TOKENS, dtype=jnp.int32)
-    lengths = jnp.stack([pool_len, val_len])
-    valid = (positions[None, :, None] < lengths[:, None, :]).astype(jnp.float32)
-    valid = jnp.repeat(valid, RANK, axis=2)
-    counts = jnp.full((8, 2 * RANK), jnp.sum(pool_len).astype(jnp.float32))
-    summed = whole(
-        pool_inputs[0], val_inputs[0], pool_top, val_top, weight[0], proj_in[0], proj_out[0], valid, counts
+    return whole(
+        pool_inputs[0], val_inputs[0], pool_top, val_top, weight[0], proj_in[0].T, proj_out[0].T, pool_len, val_len
     )
-    table = summed[:4, :32].reshape(2, 2, 32).transpose(1, 2, 0).reshape(2, 64)
-    return lax.dynamic_slice_in_dim(table, layer * 16, 16, 1)
 
 
 def solution(mesh):

time: 198 us -> 168 us (0.85)
  Pallas kernels: 189 us -> 167 us
  local copies, waits for them, and re-layouts: 6.64 us -> 1.24 us
  other arithmetic: 2.11 us -> 0 us
    pallas_call x1, Pallas kernels: 189 us -> 167 us  [whole(): pl.pallas_call(whole_kernel, out_shape=jax.ShapeDtypeStruct((2, 16), f32)...]
    unnamed x4 -> x1, local copies, waits for them, and re-layouts: 3.76 us -> 1.24 us
where the time goes in v4:
time: 168 us
  Pallas kernels  167 us (99%)
    pallas_call x1, Pallas kernels, whole(): pl.pallas_call(whole_kernel, out_shape=jax.ShapeDtypeStruct((2, 16), f32)...  167 us

profile of v4, /device:TPU:8, one launch (start us, length us, event | category | flops | bytes accessed | tf_op | source)
XLA Modules:
  0.0 167.8 jit_solution(7478197885396446561)
XLA Ops:
  0.0 166.5 %whole.1 = f32[2,16]{1,0:T(2,128)} custom-call(bf16[2,128,4096]{2,1,0:T(8,128)(2,1)} %bitcast.9, bf16[2,128,4096]{2,1,0:T(8,128)(2,1)} %bitcast.10, bf16[2,128,4096]{2,1,0:T(8,128)(2,1)} %pool_top.1, bf16[2,128,4096]{2,1,0:T(8,128)(2,1)} %val_top.1, bf16[128,4096]{1,0:T(8,128)(2,1)} %bitcast.11, bf16[64,4096]{1,0:T(8,128)(2,1)} %bitcast.12, ...), custom_call_target="tpu_custom_call" | custom-call | tf_op jit(solution)/shard_map/whole/pallas_call | solution.py:776
  166.5 1.2 copy.11

commit v5 on v4

--- a/solution.py
+++ b/solution.py
@@ -19,9 +19,10 @@
 REST = 128
 LAG_FORWARD, LAG_ROW, LAG_ROW_FORWARD, LAG_LAST, LAG_USE = 1, 2, 3, 4, 5
 LAG_GRAD = 6
+AHEAD = 3
 SLICE = 32
 PART = 16
-Q_LAG = 6
+FOLD_ONE, FOLD_TWO = 5, 7
 
 
 def silu_slope(values):
@@ -44,16 +45,28 @@
     trace_second = jnp.sum(jnp.where(lower, 0.0, on_diagonal), keepdims=True)
     damping = jnp.where(lower, trace_first, trace_second) * (0.1 / RANK)
     value = jnp.where(diagonal, pair + damping, pair)
-    for k in range(RANK):
-        left = jnp.where(
+    at = column[0:1]
+
+    def spread(k):
+        return jnp.where(
             lower,
             jnp.broadcast_to(value[:, k:k + 1], pair.shape),
             jnp.broadcast_to(value[:, RANK + k:RANK + k + 1], pair.shape),
         )
-        pivot = 1.0 / left[k:k + 1]
-        row = jnp.where(column[k:k + 1] == k, pivot, value[k:k + 1] * pivot)
-        left = jnp.where(rows == k, -1.0, left)
-        value = jnp.where((rows == k) | (column == k), 0.0, value) - left * row
+
+    for k in range(0, RANK, 2):
+        one, two = spread(k), spread(k + 1)
+        a, b = one[k:k + 1], two[k:k + 1]
+        c, d = one[k + 1:k + 2], two[k + 1:k + 2]
+        scale = 1.0 / (a * d - b * c)
+        a, b, c, d = a * scale, b * scale, c * scale, d * scale
+        upper, under = value[k:k + 1], value[k + 1:k + 2]
+        row_one = jnp.where(at == k, d, jnp.where(at == k + 1, -b, d * upper - b * under))
+        row_two = jnp.where(at == k, -c, jnp.where(at == k + 1, a, a * under - c * upper))
+        one = jnp.where(rows == k, -1.0, jnp.where(rows == k + 1, 0.0, one))
+        two = jnp.where(rows == k + 1, -1.0, jnp.where(rows == k, 0.0, two))
+        gone = (rows == k) | (rows == k + 1) | (column == k) | (column == k + 1)
+        value = jnp.where(gone, 0.0, value) - one * row_one - two * row_two
     return value
 
 
@@ -183,9 +196,11 @@
             push(ref, 0, to_along(ahead))
             push(ref, 1, to_along(behind))
 
-        def forward():
+        def forward_up():
             arrived(spot(behind, me_over, c, full), 0)
             push(spot(behind, me_over, c, (lo, mid)), 2, to_along(ahead))
+
+        def forward_down():
             arrived(spot(ahead, me_over, c, full), 1)
             push(spot(ahead, me_over, c, (mid, hi)), 3, to_along(behind))
 
@@ -195,20 +210,21 @@
             ref = spot(every, me_over, c, full)
             push(ref, 4, to_over(up))
             push(ref, 5, to_over(down))
-            push(ref, 8, sibling)
-
-        def row_forward():
+
+        def row_up():
             arrived(spot(every, down, c, full), 4)
             push(spot(slice(0, 2), down, c, full), 6, to_over(up))
+
+        def row_down():
             arrived(spot(every, up, c, full), 5)
             push(spot(slice(2, 4), up, c, full), 7, to_over(down))
-            push(spot(every, down, c, full), 9, sibling)
-            push(spot(every, up, c, full), 10, sibling)
 
         def last():
             arrived(spot(slice(0, 2), beyond, c, full), 6)
             arrived(spot(slice(2, 4), beyond, c, full), 7)
-            push(spot(every, beyond, c, full), 11, sibling)
+
+        def over_chip(slot, over):
+            return lambda: push(spot(every, over, c, full), slot, sibling)
 
         def whole():
             for slot, over in ((8, me_over), (9, down), (10, up), (11, beyond)):
@@ -227,7 +243,10 @@
             left(spot(slice(0, 2), me_over, c, full), 6)
             left(spot(slice(2, 4), me_over, c, full), 7)
 
-        return share, forward, row, row_forward, last, whole, drain
+        return (
+            [share], [forward_up, forward_down], [row, over_chip(8, me_over)],
+            [row_up, row_down, over_chip(9, down), over_chip(10, up)], [last, over_chip(11, beyond)], [whole], [drain],
+        )
 
     def weight_view(j):
         return lambda xi, zi, ci, lo, hi: held.at[j, xi, zi, ci, lo:hi]
@@ -245,9 +264,9 @@
 
     def run_stage(index):
         def stage(p):
-            one, two = list(weight_stages(p))[index]
-            one()
-            two()
+            for parts in zip(*list(weight_stages(p))[index]):
+                for part in parts:
+                    part()
         return stage
 
     def fold_view(xi, zi, ci, lo, hi):
@@ -332,8 +351,8 @@
                 share_out(2 * p, partner).start()
                 share_out(2 * p + 1, partner).start()
 
-    share_pair(0)
-    share_pair(1)
+    for pair in range(AHEAD):
+        share_pair(pair)
     for kind in range(4):
         @on(kind)
         def _():
@@ -396,6 +415,7 @@
                 gated[pl.ds(base, 64), columns(k)] = (up * silu_slope(value)).astype(bf16)
                 return carry
             lax.fori_loop(0, rows // 64, gating, 0)
+            low_two[0:rows] += transposed(grad[k, 0:rows], wide_out[1, :, columns(k)])
 
     def lower_grad(q, ready, rows):
         lower_gate(q, rows)
@@ -422,6 +442,7 @@
                     for item in proj_out_copies(kind):
                         item.start()
             folded[:, :, :, 0:RANK] = jnp.zeros((4, 4, 2, RANK, 2 * RANK), bf16)
+            low_two[...] = jnp.zeros((MAIN, 2 * RANK), f32)
 
         @pl.when(t == 1)
         def _():
@@ -434,20 +455,26 @@
                         item.wait()
 
         for index in range(4):
-            @pl.when(t == 1 + index)
+            turn_of = 1 + index + jnp.where((layer == 1) & (index > 1), 2, 0)
+
+            @pl.when(t == turn_of)
             def _():
                 block_load(block_source(index)).wait()
                 low_in[index] = transposed(block[...], wide_in[...])
-                if index < 3:
+                if index == 1:
+                    @on(1)
+                    def _():
+                        block_load(weight).start()
+
+                    @pl.when(layer != 1)
+                    def _():
+                        block_load(block_source(2)).start()
+                elif index < 3:
                     block_load(block_source(index + 1)).start()
                 else:
                     @on(3)
                     def _():
                         block_load(block_source(4)).start()
-
-                    @on(1)
-                    def _():
-                        block_load(weight).start()
         for index in range(4, 8):
             @pl.when((t == 1 + index) & (layer == 3))
             def _():
@@ -460,45 +487,49 @@
         def _():
             gate_some(3 * (t - 1), 3)
 
-        for kind in (2, 1):
-            @pl.when((t == 3) & (layer == kind))
+        for kind, when in ((2, 9), (1, 3)):
+            @pl.when((t == when) & (layer == kind))
             def _():
                 for item in proj_in_copies(kind):
                     item.wait_recv()
                 for item in proj_chip_copies(kind):
                     item.start()
 
-            @pl.when((t == 4) & (layer == kind))
+            @pl.when((t == when + 1) & (layer == kind))
             def _():
                 proj_chip_arrived(kind)
                 if kind == 1:
                     wide_out[1, RANK:2 * RANK] = wide_out[1, 0:RANK]
 
-        @pl.when((t == 5) & (layer == 1))
+        @pl.when((t == 4) & (layer == 1))
         def _():
             block_load(weight).wait()
             folded[x, z, c, RANK:2 * RANK] = transposed(wide_out[0, RANK:2 * RANK], block[...]).astype(bf16)
             mine = folded.at[x, z, c, RANK:2 * RANK]
             copy(mine, mine, fold_send.at[12], fold_recv.at[12], above).start()
+            block_load(block_source(2)).start()
 
         for index, stage in enumerate(fold_stages[:6]):
-            @pl.when((t == Q_LAG + index) & ((layer == 1) | (layer == 2)))
+            lag = jnp.where(layer == 1, FOLD_ONE, FOLD_TWO)
+
+            @pl.when((t == lag + index) & ((layer == 1) | (layer == 2)))
             def _():
                 if index == 0:
                     @on(2)
                     def _():
                         mine = folded.at[x, z, c, RANK:2 * RANK]
                         copy(mine, mine, fold_send.at[12], fold_recv.at[12], above).wait_recv()
-                stage()
+                for part in stage:
+                    part()
 
     def step(t, carry):
-        @pl.when(t + 2 < PAIRS)
-        def _():
-            share_pair(t + 2)
+        @pl.when(t + AHEAD < PAIRS)
+        def _():
+            share_pair(t + AHEAD)
         for kind, partner in ((3, above), (2, below)):
-            @pl.when((t < 4) & (layer == kind))
-            def _():
-                rest_slice(t, partner).start()
+            @pl.when((t >= 1) & (t < 5) & (layer == kind))
+            def _():
+                rest_slice(t - 1, partner).start()
 
         @pl.when((t >= 1) & (t < 9) & (layer == 1))
         def _():
@@ -539,6 +570,43 @@
         return carry
 
     lax.fori_loop(0, PAIRS + LAG_GRAD - 1, step, 0)
+
+    def drain(p, carry):
+        run_stage(6)(p)
+
+        @pl.when(layer >= 2)
+        def _():
+            share_out(2 * p, above).wait_send()
+            share_out(2 * p + 1, above).wait_send()
+        for kind, rows in ((3, MAIN), (0, REST)):
+            @on(kind)
+            def _():
+                grad_copy(2 * p, rows, above).wait_send()
+                grad_copy(2 * p + 1, rows, above).wait_send()
+        return carry
+    lax.fori_loop(0, PAIRS, drain, 0)
+
+    @pl.when(layer >= 2)
+    def _():
+        for i in range(4):
+            rest_slice(i, above).wait_send()
+
+    @on(1)
+    def _():
+        for i in range(8):
+            for source, base in main_sources:
+                main_slice(i, source, base).wait_send()
+        mine = folded.at[x, z, c, RANK:2 * RANK]
+        copy(mine, mine, fold_send.at[12], fold_recv.at[12], above).wait_send()
+
+    @pl.when((layer == 1) | (layer == 2))
+    def _():
+        fold_stages[6][0]()
+    for kind in (2, 1, 0):
+        @on(kind)
+        def _():
+            for item in proj_out_copies(kind) + proj_chip_copies(kind):
+                item.wait_send()
 
     def finish(kind, rows):
         if kind == 2:
@@ -547,29 +615,23 @@
                     main_slice(i, source, base).wait_recv()
         lower_gate(PAIRS - 1, rows)
         low_mid[0:rows] = jnp.zeros((rows, 2 * RANK), f32)
-        low_two[0:rows] = jnp.zeros((rows, 2 * RANK), f32)
-
-        def body(n, carry):
-            add_product(n, PAIRS - 1, rows)
-            low_two[0:rows] += transposed(grad[n, 0:rows], wide_out[1, :, columns(n)])
-
-            def inner(i, inner_carry):
-                base = pl.multiple_of(i * 64, 64)
-                up = grad[n, pl.ds(base, 64)].astype(f32)
-                value = second[pl.ds(base, 64), columns(n)].astype(f32)
-                low = (up + total[n, pl.ds(base, 64)]).astype(bf16)
-                first[pl.ds(base, 64), columns(n)] = low
-                grad[n, pl.ds(base, 64)] = (low.astype(f32) * silu_slope(value)).astype(bf16)
-                return inner_carry
-            lax.fori_loop(0, rows // 64, inner, 0)
-            fold = folded[n // 4, n % 4]
-            low_mid[0:rows] += (
-                transposed(first[0:rows, columns(n)], wide_out[0, :, columns(n)])
-                + transposed(grad[n, 0:rows, 0:SHARE], fold[0])
-                + transposed(grad[n, 0:rows, SHARE:COLS], fold[1])
-            )
+
+        def body(i, carry):
+            for n in (2 * i, 2 * i + 1):
+                add_product(n, PAIRS - 1, rows)
+                for base in range(0, rows, 64):
+                    part = slice(base, base + 64)
+                    up = grad[n, part].astype(f32)
+                    value = second[part, columns(n)].astype(f32)
+                    low = (up + total[n, part]).astype(bf16)
+                    first[part, columns(n)] = low
+                    grad[n, part] = (low.astype(f32) * silu_slope(value)).astype(bf16)
+                fold = folded[n // 4, n % 4]
+                left = jnp.concatenate([first[0:rows, columns(n)], grad[n, 0:rows]], 1)
+                right = jnp.concatenate([wide_out[0, :, columns(n)], fold[0], fold[1]], 1)
+                low_mid[0:rows] += transposed(left, right)
             return carry
-        lax.fori_loop(0, CHUNKS, body, 0)
+        lax.fori_loop(0, PAIRS, body, 0)
 
     wide = (RANK, 2 * RANK)
     lower = low_half(wide)
@@ -728,43 +790,6 @@
         @pl.when(layer == kind)
         def _():
             for item in lows(kind):
-                item.wait_send()
-
-    def drain(p, carry):
-        run_stage(6)(p)
-
-        @pl.when(layer >= 2)
-        def _():
-            share_out(2 * p, above).wait_send()
-            share_out(2 * p + 1, above).wait_send()
-        for kind, rows in ((3, MAIN), (0, REST)):
-            @on(kind)
-            def _():
-                grad_copy(2 * p, rows, above).wait_send()
-                grad_copy(2 * p + 1, rows, above).wait_send()
-        return carry
-    lax.fori_loop(0, PAIRS, drain, 0)
-
-    @pl.when(layer >= 2)
-    def _():
-        for i in range(4):
-            rest_slice(i, above).wait_send()
-
-    @on(1)
-    def _():
-        for i in range(8):
-            for source, base in main_sources:
-                main_slice(i, source, base).wait_send()
-        mine = folded.at[x, z, c, RANK:2 * RANK]
-        copy(mine, mine, fold_send.at[12], fold_recv.at[12], above).wait_send()
-
-    @pl.when((layer == 1) | (layer == 2))
-    def _():
-        fold_stages[6]()
-    for kind in (2, 1, 0):
-        @on(kind)
-        def _():
-            for item in proj_out_copies(kind) + proj_chip_copies(kind):
                 item.wait_send()
 
 

time: 168 us -> 159 us (0.946)
  Pallas kernels: 167 us -> 158 us
    pallas_call x1, Pallas kernels: 167 us -> 158 us  [whole(): pl.pallas_call(whole_kernel, out_shape=jax.ShapeDtypeStruct((2, 16), f32)...]
where the time goes in v5:
time: 159 us
  Pallas kernels  158 us (99%)
    pallas_call x1, Pallas kernels, whole(): pl.pallas_call(whole_kernel, out_shape=jax.ShapeDtypeStruct((2, 16), f32)...  158 us

profile of v5, /device:TPU:8, one launch (start us, length us, event | category | flops | bytes accessed | tf_op | source)
XLA Modules:
  0.0 159.3 jit_solution(11438567604112546256)
XLA Ops:
  0.0 158.0 %whole.1 = f32[2,16]{1,0:T(2,128)} custom-call(bf16[2,128,4096]{2,1,0:T(8,128)(2,1)} %bitcast.9, bf16[2,128,4096]{2,1,0:T(8,128)(2,1)} %bitcast.10, bf16[2,128,4096]{2,1,0:T(8,128)(2,1)} %pool_top.1, bf16[2,128,4096]{2,1,0:T(8,128)(2,1)} %val_top.1, bf16[128,4096]{1,0:T(8,128)(2,1)} %bitcast.11, bf16[64,4096]{1,0:T(8,128)(2,1)} %bitcast.12, ...), custom_call_target="tpu_custom_call" | custom-call | tf_op jit(solution)/shard_map/whole/pallas_call | solution.py:801
  158.0 1.2 copy.11

commit v6 on v5

--- a/solution.py
+++ b/solution.py
@@ -15,8 +15,10 @@
 COLS = WIDTH // CHUNKS
 PAIRS = CHUNKS // 2
 SHARE = 128
-MAIN = 384
-REST = 128
+MAIN = 320
+REST = 192
+FIRST = MAIN - 2 * TOKENS
+LATE = 2
 LAG_FORWARD, LAG_ROW, LAG_ROW_FORWARD, LAG_LAST, LAG_USE = 1, 2, 3, 4, 5
 LAG_GRAD = 6
 AHEAD = 3
@@ -137,16 +139,16 @@
 
     def row_loads(pool, val, target, base):
         return [
-            load(pool.at[0], target.at[0:128], base), load(pool.at[1], target.at[128:256], base + 1),
-            load(val.at[0], target.at[256:384], base + 2),
+            load(pool, target.at[0:2 * TOKENS], base),
+            load(val.at[0:FIRST], target.at[2 * TOKENS:MAIN], base + 1),
         ]
 
     def loads(kind):
         return {
             3: lambda: row_loads(pool_in, val_in, first, 0) + row_loads(pool_top, val_top, second, 3),
             2: lambda: row_loads(pool_in, val_in, first, 0),
-            1: lambda: [load(val_in.at[1], second.at[0:128], 0)],
-            0: lambda: [load(val_top.at[1], second.at[0:128], 0)],
+            1: lambda: [load(val_in.at[FIRST:2 * TOKENS], second.at[0:REST], 0)],
+            0: lambda: [load(val_top.at[FIRST:2 * TOKENS], second.at[0:REST], 0)],
         }[kind]()
 
     def rows_of(base, i):
@@ -154,16 +156,22 @@
 
     def rest_slice(i, device):
         return copy(
-            val_in.at[1, rows_of(0, i)], first.at[rows_of(0, i)], act_send.at[i], act_recv.at[i], device
+            val_in.at[rows_of(FIRST, i)], first.at[rows_of(0, i)], act_send.at[i], act_recv.at[i], device
         )
 
-    def main_slice(i, source, base):
+    def main_part(source, low, i, base):
         rows = pl.ds(pl.multiple_of(i * PART, PART), PART)
-        there = pl.ds(pl.multiple_of(base + i * PART, PART), PART)
-        index = base // PART + i
-        return copy(source.at[rows], second.at[there], act_send.at[index], act_recv.at[index], above)
-
-    main_sources = ((pool_in.at[0], 0), (pool_in.at[1], 128), (val_in.at[0], 256))
+        there = pl.ds(pl.multiple_of(low + i * PART, PART), PART)
+        return copy(source.at[rows], second.at[there], act_send.at[base + i], act_recv.at[base + i], above)
+
+    def pool_part(i):
+        return main_part(pool_in, 0, i, 0)
+
+    def val_part(i):
+        return main_part(val_in, 2 * TOKENS, i, 2 * TOKENS // PART)
+
+    def main_parts():
+        return [pool_part(i) for i in range(2 * TOKENS // PART)] + [val_part(i) for i in range(FIRST // PART)]
 
     def gather_stages(j, view, flip, sems, part):
         send_j, recv_j = sems
@@ -331,8 +339,8 @@
         return [load(proj_in, wide_in.at[i * RANK:(i + 1) * RANK], 10 + i) for i in range(2)]
 
     def block_source(index):
-        return (pool_in.at[0], pool_in.at[1], val_in.at[0], val_in.at[1],
-                pool_top.at[0], pool_top.at[1], val_top.at[0], val_top.at[1])[index]
+        half = slice(index % 2 * TOKENS, (index % 2 + 1) * TOKENS)
+        return (pool_in, val_in, pool_top, val_top)[index // 2].at[half]
 
     def block_load(source):
         return load(source, block, 7)
@@ -485,7 +493,7 @@
 
         @pl.when((t >= 1) & (t < 5) & (layer == 3))
         def _():
-            gate_some(3 * (t - 1), 3)
+            gate_some(3 * (t - 1), jnp.minimum(3, MAIN // 32 - 3 * (t - 1)))
 
         for kind, when in ((2, 9), (1, 3)):
             @pl.when((t == when) & (layer == kind))
@@ -527,14 +535,18 @@
         def _():
             share_pair(t + AHEAD)
         for kind, partner in ((3, above), (2, below)):
-            @pl.when((t >= 1) & (t < 5) & (layer == kind))
+            @pl.when((t >= 1) & (t <= REST // SLICE) & (layer == kind))
             def _():
                 rest_slice(t - 1, partner).start()
 
         @pl.when((t >= 1) & (t < 9) & (layer == 1))
         def _():
-            for source, base in main_sources:
-                main_slice(t - 1, source, base).start()
+            pool_part(2 * (t - 1)).start()
+            pool_part(2 * (t - 1) + 1).start()
+
+            @pl.when(t % 2 == 1)
+            def _():
+                val_part((t - 1) // 2).start()
 
         when_in(t, 0, have_share)
         for lag, index in ((0, 0), (LAG_FORWARD, 1), (LAG_ROW, 2), (LAG_ROW_FORWARD, 3), (LAG_LAST, 4)):
@@ -542,31 +554,46 @@
         early(t)
         when_in(t, LAG_USE, run_stage(5))
 
-        @pl.when((t == LAG_USE) & (layer < 2))
-        def _():
-            for i in range(4):
+        @pl.when((t == LAG_USE + LATE) & (layer < 2))
+        def _():
+            for i in range(REST // SLICE):
                 rest_slice(i, above).wait_recv()
 
             @on(0)
             def _():
                 gate_some(0, REST // 32)
 
-        for kind, rows, target in ((3, MAIN, below), (0, REST, above)):
-            @pl.when((layer == kind) & (t >= LAG_USE) & (t < PAIRS + LAG_USE))
+                def body(j, inner_carry):
+                    upper_chunk(j, REST, above)
+                    return inner_carry
+                lax.fori_loop(0, 2 * LATE, body, 0)
+
+        for kind, rows, target, begin in ((3, MAIN, below, LAG_USE), (0, REST, above, LAG_USE + LATE)):
+            @pl.when((layer == kind) & (t >= begin) & (t < PAIRS + LAG_USE))
             def _():
                 upper_chunk(2 * (t - LAG_USE), rows, target)
                 upper_chunk(2 * (t - LAG_USE) + 1, rows, target)
 
         whole = jnp.minimum(2 * (t - LAG_USE) + 2, CHUNKS)
-        for kind, rows in ((2, MAIN), (1, REST)):
+        begin_rest = LAG_GRAD + LATE
+        ready_rest = jnp.where(t <= begin_rest, 0, jnp.where(t < begin_rest + LATE, 2 * (t - begin_rest), t - LAG_GRAD))
+        for kind, rows, ready in ((2, MAIN, jnp.maximum(t - LAG_GRAD, 0)), (1, REST, ready_rest)):
             @pl.when((layer == kind) & (t >= LAG_USE) & (t < PAIRS + LAG_USE))
             def _():
-                ready = jnp.maximum(t - LAG_GRAD, 0)
                 lower_weight(2 * (t - LAG_USE), ready, rows)
 
-            @pl.when((layer == kind) & (t >= LAG_GRAD) & (t < PAIRS + LAG_GRAD - 1))
-            def _():
-                lower_grad(t - LAG_GRAD, whole, rows)
+        @pl.when((layer == 2) & (t >= LAG_GRAD) & (t < PAIRS + LAG_GRAD - 1))
+        def _():
+            lower_grad(t - LAG_GRAD, whole, MAIN)
+
+        @pl.when((layer == 1) & (t >= begin_rest) & (t < begin_rest + LATE))
+        def _():
+            lower_grad(2 * (t - begin_rest), whole, REST)
+            lower_grad(2 * (t - begin_rest) + 1, whole, REST)
+
+        @pl.when((layer == 1) & (t >= begin_rest + LATE) & (t < PAIRS + LAG_GRAD - 1))
+        def _():
+            lower_grad(t - LAG_GRAD, whole, REST)
         return carry
 
     lax.fori_loop(0, PAIRS + LAG_GRAD - 1, step, 0)
@@ -588,14 +615,13 @@
 
     @pl.when(layer >= 2)
     def _():
-        for i in range(4):
+        for i in range(REST // SLICE):
             rest_slice(i, above).wait_send()
 
     @on(1)
     def _():
-        for i in range(8):
-            for source, base in main_sources:
-                main_slice(i, source, base).wait_send()
+        for item in main_parts():
+            item.wait_send()
         mine = folded.at[x, z, c, RANK:2 * RANK]
         copy(mine, mine, fold_send.at[12], fold_recv.at[12], above).wait_send()
 
@@ -610,9 +636,8 @@
 
     def finish(kind, rows):
         if kind == 2:
-            for i in range(8):
-                for source, base in main_sources:
-                    main_slice(i, source, base).wait_recv()
+            for item in main_parts():
+                item.wait_recv()
         lower_gate(PAIRS - 1, rows)
         low_mid[0:rows] = jnp.zeros((rows, 2 * RANK), f32)
 
@@ -658,8 +683,11 @@
     @on(2)
     def _():
         finish(2, MAIN)
-        mid = [low_mid[i * TOKENS:(i + 1) * TOKENS] for i in range(3)]
-        two = [low_two[i * TOKENS:(i + 1) * TOKENS] for i in range(3)]
+        def short(ref):
+            return jnp.concatenate([ref[2 * TOKENS:MAIN], jnp.zeros((TOKENS - FIRST, 2 * RANK), f32)], 0)
+
+        mid = [low_mid[0:TOKENS], low_mid[TOKENS:2 * TOKENS], short(low_mid)]
+        two = [low_two[0:TOKENS], low_two[TOKENS:2 * TOKENS], short(low_two)]
         put(1, 0, jnp.where(lower_rows, mid[0], swap(mid[1])), 0)
         put(1, 1, jnp.where(lower_rows, mid[2], 0.0), 1)
         put(0, 0, jnp.where(lower_rows, swap(mid[0]), mid[1]), 0)
@@ -670,10 +698,17 @@
     @on(1)
     def _():
         finish(1, REST)
-        mid, two = low_mid[0:TOKENS], low_two[0:TOKENS]
-        put(0, 1, jnp.where(lower_rows, 0.0, mid), 1)
-        put(2, 1, jnp.where(lower_rows, 0.0, two), 1)
-        landed[2] = (jnp.where(lower_rows, 0.0, swap(mid)) * valid[1]).astype(bf16)
+        def split(ref):
+            other_tokens = REST - TOKENS
+            return (
+                jnp.concatenate([jnp.zeros((TOKENS - other_tokens, 2 * RANK), f32), ref[0:other_tokens]], 0),
+                ref[other_tokens:REST],
+            )
+
+        one, two = split(low_mid), split(low_two)
+        put(0, 1, jnp.where(lower_rows, swap(one[0]), one[1]), 1)
+        put(2, 1, jnp.where(lower_rows, two[0], two[1]), 1)
+        landed[2] = (jnp.where(lower_rows, one[0], swap(one[1])) * valid[1]).astype(bf16)
 
     def low(source, slot, plane):
         return copy(source, landed.at[slot], low_send.at[slot + 3 * plane], low_recv.at[slot], {"layer": plane})
@@ -839,7 +874,7 @@
     pool_inputs, val_inputs, pool_top, val_top, weight, proj_in, proj_out, pool_len, val_len
 ):
     return whole(
-        pool_inputs[0], val_inputs[0], pool_top, val_top, weight[0], proj_in[0].T, proj_out[0].T, pool_len, val_len
+        *(rows.reshape(-1, WIDTH) for rows in (pool_inputs[0], val_inputs[0], pool_top, val_top)), weight[0], proj_in[0].T, proj_out[0].T, pool_len, val_len
     )
 
 

time: 159 us -> 154 us (0.969)
  Pallas kernels: 158 us -> 153 us
    pallas_call x1, Pallas kernels: 158 us -> 153 us  [whole(): pl.pallas_call(whole_kernel, out_shape=jax.ShapeDtypeStruct((2, 16), f32)...]
where the time goes in v6:
time: 154 us
  Pallas kernels  153 us (99%)
    pallas_call x1, Pallas kernels, whole(): pl.pallas_call(whole_kernel, out_shape=jax.ShapeDtypeStruct((2, 16), f32)...  153 us

profile of v6, /device:TPU:8, one launch (start us, length us, event | category | flops | bytes accessed | tf_op | source)
XLA Modules:
  0.0 154.0 jit_solution(7719205453805934261)
XLA Ops:
  0.0 152.7 %whole.1 = f32[2,16]{1,0:T(2,128)} custom-call(bf16[256,4096]{1,0:T(8,128)(2,1)} %bitcast.11, bf16[256,4096]{1,0:T(8,128)(2,1)} %bitcast.12, bf16[256,4096]{1,0:T(8,128)(2,1)} %bitcast.13, bf16[256,4096]{1,0:T(8,128)(2,1)} %bitcast.14, bf16[128,4096]{1,0:T(8,128)(2,1)} %bitcast.15, bf16[64,4096]{1,0:T(8,128)(2,1)} %bitcast.16, bf16[64,4096]{1,0:T(8,128)(2,1)} %bitcast.17, ...), custom_call_target="tpu_custom_call" | custom-call | tf_op jit(solution)/shard_map/whole/pallas_call | solution.py:836
  152.7 1.2 copy.11

commit v7 on v6

--- a/solution.py
+++ b/solution.py
@@ -45,8 +45,8 @@
     on_diagonal = jnp.where(diagonal, pair, 0.0)
     trace_first = jnp.sum(jnp.where(lower, on_diagonal, 0.0), keepdims=True)
     trace_second = jnp.sum(jnp.where(lower, 0.0, on_diagonal), keepdims=True)
-    damping = jnp.where(lower, trace_first, trace_second) * (0.1 / RANK)
-    value = jnp.where(diagonal, pair + damping, pair)
+    scale_back = RANK / jnp.where(lower, trace_first, trace_second)
+    value = jnp.where(diagonal, pair * scale_back + 0.1, pair * scale_back)
     at = column[0:1]
 
     def spread(k):
@@ -69,7 +69,7 @@
         two = jnp.where(rows == k + 1, -1.0, jnp.where(rows == k, 0.0, two))
         gone = (rows == k) | (rows == k + 1) | (column == k) | (column == k + 1)
         value = jnp.where(gone, 0.0, value) - one * row_one - two * row_two
-    return value
+    return value * scale_back
 
 
 def whole_kernel(
@@ -715,8 +715,8 @@
 
     def lows(kind):
         if kind == 2:
-            return [low(outgoing.at[1, 0], 0, 1), low(outgoing.at[1, 1], 1, 1),
-                    low(outgoing.at[0, 0], 0, 0), low(outgoing.at[0, 1], 1, 0)]
+            return [low(outgoing.at[0, 0], 0, 0), low(outgoing.at[0, 1], 1, 0),
+                    low(outgoing.at[1, 0], 0, 1), low(outgoing.at[1, 1], 1, 1)]
         if kind == 1:
             return [low(outgoing.at[0, 1], 2, 0), low(outgoing.at[2, 1], 2, 2)]
         return []

time: 154 us -> 154 us (level)
  no operation moved by 1% of the time
where the time goes in v7:
time: 154 us
  Pallas kernels  153 us (99%)
    pallas_call x1, Pallas kernels, whole(): pl.pallas_call(whole_kernel, out_shape=jax.ShapeDtypeStruct((2, 16), f32)...  153 us

profile of v7, /device:TPU:8, one launch (start us, length us, event | category | flops | bytes accessed | tf_op | source)
XLA Modules:
  0.0 154.0 jit_solution(1393474847041898069)
XLA Ops:
  0.0 152.7 %whole.1 = f32[2,16]{1,0:T(2,128)} custom-call(bf16[256,4096]{1,0:T(8,128)(2,1)} %bitcast.11, bf16[256,4096]{1,0:T(8,128)(2,1)} %bitcast.12, bf16[256,4096]{1,0:T(8,128)(2,1)} %bitcast.13, bf16[256,4096]{1,0:T(8,128)(2,1)} %bitcast.14, bf16[128,4096]{1,0:T(8,128)(2,1)} %bitcast.15, bf16[64,4096]{1,0:T(8,128)(2,1)} %bitcast.16, bf16[64,4096]{1,0:T(8,128)(2,1)} %bitcast.17, ...), custom_call_target="tpu_custom_call" | custom-call | tf_op jit(solution)/shard_map/whole/pallas_call | solution.py:836
  152.7 1.2 copy.11

commit v8 on v7

--- a/solution.py
+++ b/solution.py
@@ -173,7 +173,7 @@
     def main_parts():
         return [pool_part(i) for i in range(2 * TOKENS // PART)] + [val_part(i) for i in range(FIRST // PART)]
 
-    def gather_stages(j, view, flip, sems, part):
+    def gather_stages(j, view, flip, sems, part, apart):
         send_j, recv_j = sems
         ahead, behind, far = (zp, zm, zo) if flip else (xp, xm, xo)
         up, down, beyond = (xp, xm, xo) if flip else (zp, zm, zo)
@@ -232,11 +232,20 @@
             arrived(spot(slice(2, 4), beyond, c, full), 7)
 
         def over_chip(slot, over):
-            return lambda: push(spot(every, over, c, full), slot, sibling)
+            def row_push():
+                pl.when(apart)(lambda: push(spot(every, over, c, full), slot, sibling))
+            return row_push
+
+        def over_chip_all():
+            pl.when(jnp.logical_not(apart))(lambda: push(spot(every, every, c, full), 8, sibling))
 
         def whole():
-            for slot, over in ((8, me_over), (9, down), (10, up), (11, beyond)):
-                arrived(spot(every, over, other, full), slot)
+            @pl.when(apart)
+            def _():
+                for slot, over in ((8, me_over), (9, down), (10, up), (11, beyond)):
+                    arrived(spot(every, over, other, full), slot)
+
+            pl.when(jnp.logical_not(apart))(lambda: arrived(spot(every, every, other, full), 8))
 
         def drain():
             def left(ref, slot):
@@ -246,14 +255,21 @@
                 left(spot(me_along, me_over, c, full), slot)
             left(spot(me_along, me_over, c, (lo, mid)), 2)
             left(spot(me_along, me_over, c, (mid, hi)), 3)
-            for slot in (4, 5, 8, 9, 10, 11):
+            for slot in (4, 5):
                 left(spot(every, me_over, c, full), slot)
+
+            @pl.when(apart)
+            def _():
+                for slot in (8, 9, 10, 11):
+                    left(spot(every, me_over, c, full), slot)
+
+            pl.when(jnp.logical_not(apart))(lambda: left(spot(every, every, c, full), 8))
             left(spot(slice(0, 2), me_over, c, full), 6)
             left(spot(slice(2, 4), me_over, c, full), 7)
 
         return (
             [share], [forward_up, forward_down], [row, over_chip(8, me_over)],
-            [row_up, row_down, over_chip(9, down), over_chip(10, up)], [last, over_chip(11, beyond)], [whole], [drain],
+            [row_up, row_down, over_chip(9, down), over_chip(10, up)], [last, over_chip(11, beyond), over_chip_all], [whole], [drain],
         )
 
     def weight_view(j):
@@ -266,8 +282,8 @@
         a, b = 2 * p, 2 * p + 1
         part = (0, SHARE // 2, SHARE)
         return zip(
-            gather_stages(a, weight_view(a), False, weight_sems, part),
-            gather_stages(b, weight_view(b), True, weight_sems, part),
+            gather_stages(a, weight_view(a), False, weight_sems, part, p == PAIRS - 1),
+            gather_stages(b, weight_view(b), True, weight_sems, part, p == PAIRS - 1),
         )
 
     def run_stage(index):
@@ -280,7 +296,7 @@
     def fold_view(xi, zi, ci, lo, hi):
         return folded.at[xi, zi, ci, lo:hi]
 
-    fold_stages = gather_stages(0, fold_view, False, fold_sems, (RANK, RANK + RANK // 2, 2 * RANK))
+    fold_stages = gather_stages(0, fold_view, False, fold_sems, (RANK, RANK + RANK // 2, 2 * RANK), layer >= 0)
 
     def have_share(p):
         for j in (2 * p, 2 * p + 1):

time: 154 us -> 154 us (level)
  no operation moved by 1% of the time
where the time goes in v8:
time: 154 us
  Pallas kernels  153 us (99%)
    pallas_call x1, Pallas kernels, whole(): pl.pallas_call(whole_kernel, out_shape=jax.ShapeDtypeStruct((2, 16), f32)...  153 us

profile of v8, /device:TPU:8, one launch (start us, length us, event | category | flops | bytes accessed | tf_op | source)
XLA Modules:
  0.0 154.0 jit_solution(372217917650262373)
XLA Ops:
  0.0 152.7 %whole.1 = f32[2,16]{1,0:T(2,128)} custom-call(bf16[256,4096]{1,0:T(8,128)(2,1)} %bitcast.11, bf16[256,4096]{1,0:T(8,128)(2,1)} %bitcast.12, bf16[256,4096]{1,0:T(8,128)(2,1)} %bitcast.13, bf16[256,4096]{1,0:T(8,128)(2,1)} %bitcast.14, bf16[128,4096]{1,0:T(8,128)(2,1)} %bitcast.15, bf16[64,4096]{1,0:T(8,128)(2,1)} %bitcast.16, bf16[64,4096]{1,0:T(8,128)(2,1)} %bitcast.17, ...), custom_call_target="tpu_custom_call" | custom-call | tf_op jit(solution)/shard_map/whole/pallas_call | solution.py:852
  152.7 1.2 copy.11
